TPU v7x, 128 devices: a whole 4x4x4 slice. The times are simulated.
128 devices in a mesh: row: 8 (over z_hi, y), col: 16 (over z_lo, x, core).
Axes of the slice: x: 4, y: 4, z: 4 (z_hi: 2, z_lo: 2; z = z_hi * 2 + z_lo), core: 2. Of those that a mesh axis runs over, the one named last changes fastest.
Arguments:
- inputs: bfloat16 [1536, 7168], P('col', 'row'), may hold values from -6 to 6
- teacher: bfloat16 [1536, 7168], P('col', 'row'), may hold values from -6 to 6
- weight_in: bfloat16 [7168, 18432], P('row', 'col'), may hold values from -0.0625 to 0.0625
- weight_out: bfloat16 [18432, 7168], P('col', 'row'), may hold values from -0.046875 to 0.046875
Outputs:
- grad_inputs: bfloat16 [1536, 7168], P('col', 'row')
- grad_weight_in: bfloat16 [7168, 18432], P('row', 'col')
- grad_weight_out: bfloat16 [18432, 7168], P('col', 'row')
All inputs are finite; a program needn't handle non-finite values.
Results may differ from a plain program's by a relative error of at most 0.008.
Values may be sent and summed in bfloat16 or wider, within the bound.
A program may use at most 128 MiB of HBM per device.

v0:
```python
import math

import jax
import jax.numpy as jnp
from jax import lax
from jax.sharding import PartitionSpec as P


def gelu_value(hidden):
    return 0.5 * hidden * (1.0 + jax.scipy.special.erf(hidden / math.sqrt(2.0)))


def gelu_slope(hidden):
    cumul = 0.5 * (1.0 + jax.scipy.special.erf(hidden / math.sqrt(2.0)))
    return cumul + hidden * jnp.exp(-0.5 * hidden * hidden) / math.sqrt(2.0 * math.pi)


def contract_rows(left, right):
    return lax.dot_general(
        left, right, (((0,), (0,)), ((), ())), preferred_element_type=jnp.float32
    )


def contract_cols(left, right):
    return lax.dot_general(
        left, right, (((1,), (1,)), ((), ())), preferred_element_type=jnp.float32
    )


def shards(inputs, teacher, weight_in, weight_out):
    all_inputs = lax.all_gather(inputs, "col", axis=0, tiled=True)
    block = all_inputs
    hidden = lax.psum_scatter(
        jnp.dot(block, weight_in, preferred_element_type=jnp.float32),
        "row",
        scatter_dimension=0,
        tiled=True,
    )
    all_act = lax.all_gather(gelu_value(hidden).astype(jnp.bfloat16), "row", axis=0, tiled=True)
    block = all_act
    student = lax.psum_scatter(
        jnp.dot(block, weight_out, preferred_element_type=jnp.float32),
        "col",
        scatter_dimension=0,
        tiled=True,
    )
    d_out = (0.125 * (student - teacher.astype(jnp.float32))).astype(jnp.bfloat16)
    all_dout = lax.all_gather(d_out, "col", axis=0, tiled=True)
    grad_weight_out = contract_rows(all_act, all_dout).astype(jnp.bfloat16)
    block = all_dout
    d_act = lax.psum_scatter(
        contract_cols(block, weight_out), "row", scatter_dimension=0, tiled=True
    )
    all_dhidden = lax.all_gather(
        (d_act * gelu_slope(hidden)).astype(jnp.bfloat16), "row", axis=0, tiled=True
    )
    grad_weight_in = contract_rows(all_inputs, all_dhidden).astype(jnp.bfloat16)
    block = all_dhidden
    grad_inputs = lax.psum_scatter(
        contract_cols(block, weight_in), "col", scatter_dimension=0, tiled=True
    ).astype(jnp.bfloat16)
    return (grad_inputs, grad_weight_in, grad_weight_out)


def solution(mesh):
    placed = (P("col", "row"), P("col", "row"), P("row", "col"), P("col", "row"))
    return jax.shard_map(
        shards,
        mesh=mesh,
        in_specs=placed,
        out_specs=(P("col", "row"), P("row", "col"), P("col", "row")),
        check_vma=False,
    )
```

profile of v0, /device:TPU:0, one launch (start us, length us, event | category | flops | bytes accessed | tf_op | source)
XLA Modules:
  0.0 609.5 jit_solution(13347695101357593946)
XLA Ops:
  7.2 0.7 all-gather.5.cloned.1.call-update
  8.0 39.4 %all-gather.5.cloned.1.call-done = bf16[1536,896]{1,0:T(8,128)(2,1)} async-done(((bf16[96,896]{1,0:T(8,128)(2,1)}), bf16[1536,896]{1,0:T(8,128)(2,1)}) %all-gather.5.cloned.1.call-update) | async-done | bytes 2752528 | tf_op jit(solution)/shard_map/all_gather | solution.py:31
  47.3 9.5 %fusion.7 = f32[1536,1152]{1,0:T(8,128)} fusion(bf16[1536,896]{1,0:T(8,128)(2,1)} %all-gather.5.cloned.1.call-done, bf16[896,1152]{1,0:T(8,128)(2,1)} %param.6), kind=kOutput, calls=%fused_computation.13 | convolution fusion | flops 3170893824 | bytes 11894784 | tf_op jit(solution)/shard_map/dot_general | solution.py:34
  56.9 106.2 %reduce-scatter.5.cloned.1.call-done = f32[192,1152]{1,0:T(8,128)} async-done(((f32[1536,1152]{1,0:T(8,128)}), f32[192,1152]{1,0:T(8,128)}) %reduce-scatter.5.cloned.1.call-update) | async-done | bytes 884752 | tf_op jit(solution)/shard_map/reduce_scatter | solution.py:33
  163.2 2.1 multiply_convert_fusion
  165.3 0.0 reduce-scatter.7.cloned.1.call-start
  165.3 65.4 %all-gather.7.cloned.1.call-done = bf16[1536,1152]{1,0:T(8,128)(2,1)} async-done(((bf16[192,1152]{1,0:T(8,128)(2,1)}), bf16[1536,1152]{1,0:T(8,128)(2,1)}) %all-gather.7.cloned.1.call-update) | async-done | bytes 3538960 | tf_op jit(solution)/shard_map/all_gather | solution.py:39
  230.7 8.0 %fusion.8 = f32[1536,896]{1,0:T(8,128)} fusion(bf16[1536,1152]{1,0:T(8,128)(2,1)} %all-gather.7.cloned.1.call-done, bf16[1152,896]{1,0:T(8,128)(2,1)S(1)} %copy-done), kind=kOutput, calls=%fused_computation.14 | convolution fusion | flops 3170893824 | bytes 11108352 | tf_op jit(solution)/shard_map/dot_general | solution.py:42
  238.7 0.0 all-gather.9.cloned.1.call-start
  238.8 67.2 %reduce-scatter.7.cloned.1.call-done = f32[96,896]{1,0:T(8,128)} async-done(((f32[1536,896]{1,0:T(8,128)}), f32[96,896]{1,0:T(8,128)}) %reduce-scatter.7.cloned.1.call-update) | async-done | bytes 344080 | tf_op jit(solution)/shard_map/reduce_scatter | solution.py:41
  305.9 1.7 multiply_convert_fusion.1
  307.7 34.2 %all-gather.9.cloned.1.call-done = bf16[1536,896]{1,0:T(8,128)(2,1)} async-done(((bf16[96,896]{1,0:T(8,128)(2,1)}), bf16[1536,896]{1,0:T(8,128)(2,1)}) %all-gather.9.cloned.1.call-update) | async-done | bytes 2752528 | tf_op jit(solution)/shard_map/all_gather | solution.py:48
  341.9 8.9 %fusion.9 = f32[1536,1152]{1,0:T(8,128)} fusion(bf16[1536,896]{1,0:T(8,128)(2,1)} %all-gather.9.cloned.1.call-done, bf16[1152,896]{1,0:T(8,128)(2,1)S(1)} %copy-done), kind=kOutput, calls=%fused_computation.15 | convolution fusion | flops 3170893824 | bytes 11894784 | tf_op jit(solution)/shard_map/dot_general | solution.py:25
  350.8 0.0 all-gather.11.cloned.1.call-start
  350.8 106.1 %reduce-scatter.9.cloned.1.call-done = f32[192,1152]{1,0:T(8,128)} async-done(((f32[1536,1152]{1,0:T(8,128)}), f32[192,1152]{1,0:T(8,128)}) %reduce-scatter.9.cloned.1.call-update) | async-done | bytes 884752 | tf_op jit(solution)/shard_map/reduce_scatter | solution.py:51
  456.9 2.3 fusion.6
  459.2 0.2 reduce-scatter.11.cloned.1.call-start
  459.5 65.0 %all-gather.11.cloned.1.call-done = bf16[1536,1152]{1,0:T(8,128)(2,1)} async-done(((bf16[192,1152]{1,0:T(8,128)(2,1)}), bf16[1536,1152]{1,0:T(8,128)(2,1)}) %all-gather.11.cloned.1.call-update) | async-done | bytes 3538960 | tf_op jit(solution)/shard_map/all_gather | solution.py:54
  524.5 9.3 %fusion.10 = f32[1536,896]{1,0:T(8,128)} fusion(bf16[1536,1152]{1,0:T(8,128)(2,1)} %all-gather.11.cloned.1.call-done, bf16[896,1152]{1,0:T(8,128)(2,1)} %param.6), kind=kOutput, calls=%fused_computation.16 | convolution fusion | flops 3170893824 | bytes 11108352 | tf_op jit(solution)/shard_map/dot_general | solution.py:25
  533.8 8.2 %convolution_convert_fusion = bf16[1152,896]{1,0:T(8,128)(2,1)} fusion(bf16[1536,1152]{1,0:T(8,128)(2,1)} %all-gather.7.cloned.1.call-done, bf16[1536,896]{1,0:T(8,128)(2,1)} %all-gather.9.cloned.1.call-done), kind=kOutput, calls=%fused_computation | convolution fusion | flops 3171926016 | bytes 8355840 | tf_op jit(solution)/shard_map/dot_general | solution.py:19
  541.9 5.1 fusion
  547.0 4.1 copy.7
  551.1 49.8 %reduce-scatter.11.cloned.1.call-done = f32[96,896]{1,0:T(8,128)} async-done(((f32[1536,896]{1,0:T(8,128)}), f32[96,896]{1,0:T(8,128)}) %reduce-scatter.11.cloned.1.call-update) | async-done | bytes 344080 | tf_op jit(solution)/shard_map/reduce_scatter | solution.py:59
  601.0 1.7 convert_element_type.28
  (21 shorter events, 0.3 us)
Async XLA Ops:
  7.2 223.6 %copy-start = (bf16[1152,896]{1,0:T(8,128)(2,1)S(1)}, bf16[1152,896]{1,0:T(8,128)(2,1)}, u32[]{:S(2)}) copy-start(bf16[1152,896]{1,0:T(8,128)(2,1)} %param.7) | copy-start | bytes 6193156
  7.2 40.2 %all-gather.5.cloned.1.call-start = ((), (), s32[]{:S(2)}) async-start(), calls=%async_computation.4 | async-start | bytes 2924544 | tf_op jit(solution)/shard_map/all_gather | solution.py:31
  7.9 155.2 %reduce-scatter.5.cloned.1.call-start = ((), (), s32[]{:S(2)}) async-start(), calls=%async_computation.5 | async-start | bytes 7962624 | tf_op jit(solution)/shard_map/reduce_scatter | solution.py:33
  56.9 173.9 %all-gather.7.cloned.1.call-start = ((), (), s32[]{:S(2)}) async-start(), calls=%async_computation.6 | async-start | bytes 3981312 | tf_op jit(solution)/shard_map/all_gather | solution.py:39
  165.3 140.7 %reduce-scatter.7.cloned.1.call-start = ((), (), s32[]{:S(2)}) async-start(), calls=%async_computation.7 | async-start | bytes 5849088 | tf_op jit(solution)/shard_map/reduce_scatter | solution.py:41
  238.7 67.3 %copy-start.2 = (bf16[96,896]{1,0:T(8,128)(2,1)S(1)}, bf16[96,896]{1,0:T(8,128)(2,1)}, u32[]{:S(2)}) copy-start(bf16[96,896]{1,0:T(8,128)(2,1)} %param.5) | copy-start | bytes 516100
  238.7 103.1 %all-gather.9.cloned.1.call-start = ((), (), s32[]{:S(2)}) async-start(), calls=%async_computation.8 | async-start | bytes 2924544 | tf_op jit(solution)/shard_map/all_gather | solution.py:48
  307.7 149.3 %reduce-scatter.9.cloned.1.call-start = ((), (), s32[]{:S(2)}) async-start(), calls=%async_computation.9 | async-start | bytes 7962624 | tf_op jit(solution)/shard_map/reduce_scatter | solution.py:51
  350.7 106.2 %copy-start.1 = (f32[192,1152]{1,0:T(8,128)S(1)}, f32[192,1152]{1,0:T(8,128)}, u32[]{:S(2)}) copy-start(f32[192,1152]{1,0:T(8,128)} %reduce-scatter.5.cloned.1.call-done) | copy-start | bytes 2654212
  350.8 173.7 %all-gather.11.cloned.1.call-start = ((), (), s32[]{:S(2)}) async-start(), calls=%async_computation.10 | async-start | bytes 3981312 | tf_op jit(solution)/shard_map/all_gather | solution.py:54
  459.2 141.7 %reduce-scatter.11.cloned.1.call-start = ((), (), s32[]{:S(2)}) async-start(), calls=%async_computation.11 | async-start | bytes 5849088 | tf_op jit(solution)/shard_map/reduce_scatter | solution.py:59
  533.8 8.2 %copy-start.3 = (bf16[1536,1152]{1,0:T(8,128)(2,1)S(1)}, bf16[1536,1152]{1,0:T(8,128)(2,1)}, u32[]{:S(2)}) copy-start(bf16[1536,1152]{1,0:T(8,128)(2,1)} %all-gather.11.cloned.1.call-done) | copy-start | bytes 10616836
  533.8 8.2 %copy-start.4 = (bf16[1536,896]{1,0:T(8,128)(2,1)S(1)}, bf16[1536,896]{1,0:T(8,128)(2,1)}, u32[]{:S(2)}) copy-start(bf16[1536,896]{1,0:T(8,128)(2,1)} %all-gather.5.cloned.1.call-done) | copy-start | bytes 8257540
Sparse Core Ops, SparseCore 0:
  9.7 37.5 all-gather.4
  57.0 106.1 reduce-scatter.4
  166.3 64.3 all-gather.6
  238.8 67.0 reduce-scatter.6
  308.1 33.7 all-gather.8
  350.9 105.9 reduce-scatter.8
  460.1 64.3 all-gather.10
  533.9 67.0 reduce-scatter.10
where the time goes:
time: 610 us; the launch traced here: 609 us
  waiting for transfers between devices  534 us (88%)
  matrix products  48.9 us (8%)
  between operations  14.2 us (2%)
  other arithmetic  7.74 us (1%)
    reduce_scatter x1, waiting for transfers between devices, shards(): lax.psum_scatter(jnp.dot(block, weight_in, preferred_element_type=jnp.flo...  106 us
    reduce_scatter x1, waiting for transfers between devices, shards(): lax.psum_scatter(contract_cols(block, weight_out), 'row', scatter_dimensi...  106 us
    reduce_scatter x1, waiting for transfers between devices, shards(): lax.psum_scatter(jnp.dot(block, weight_out, preferred_element_type=jnp.fl...  67.2 us
    all_gather x1, waiting for transfers between devices, shards(): lax.all_gather(gelu_value(hidden).astype(jnp.bfloat16), 'row', axis=0, ti...  65.4 us
    all_gather x1, waiting for transfers between devices, shards(): lax.all_gather((d_act * gelu_slope(hidden)).astype(jnp.bfloat16), 'row',...  65 us
    reduce_scatter x1, waiting for transfers between devices, shards(): lax.psum_scatter(contract_cols(block, weight_in), 'col', scatter_dimensio...  49.8 us
    all_gather x1, waiting for transfers between devices, shards(): all_inputs = lax.all_gather(inputs, 'col', axis=0, tiled=True)  39.4 us
    all_gather x1, waiting for transfers between devices, shards(): all_dout = lax.all_gather(d_out, 'col', axis=0, tiled=True)  34.2 us
  transfers between devices with their start and end apart: 8, of which 8 were waited for; matrix products, arithmetic and copies ran while one was open for 3% of the time, Pallas kernels for 0%

commit v1 on v0

v1 whole, which is shorter than its diff:
```python
import math

import jax
import jax.numpy as jnp
from jax import lax
from jax.experimental import pallas as pl
from jax.experimental.pallas import tpu as pltpu
from jax.sharding import PartitionSpec as P

MESH = pl.DeviceIdType.MESH
F32 = jnp.float32
BF16 = jnp.bfloat16

K = 2
RB = 96 // K
D = 896
H = 1152
HALF = 8 * RB

ORDER = (
    "A0", "B0", "A1", "B1", "A2", "B2", "A3", "B3", "A4", "A5",
    "A6", "B4", "A7", "B5", "B6", "A8", "B7", "A9", "B8", "B9",
    "A10", "G", "B10", "A11", "B11", "A12", "A13", "A14", "B12", "A15",
    "B13", "W", "B14", "B15",
)


def gelu_value(hidden):
    return 0.5 * hidden * (1.0 + lax.erf(hidden * (1.0 / math.sqrt(2.0))))


def gelu_slope(hidden):
    cumul = 0.5 * (1.0 + lax.erf(hidden * (1.0 / math.sqrt(2.0))))
    return cumul + hidden * jnp.exp(-0.5 * hidden * hidden) * (1.0 / math.sqrt(2.0 * math.pi))


def kernel(
    x_hbm, t_hbm, wi_hbm, wo_hbm, gi_hbm, gwi_hbm, gwo_hbm,
    wi, wo, tch, gi, gwi, gwo, hid,
    hp, hz, hy, hz2, hy2, ag, xg, sp, sc, sr,
    lsem, osem, cs, cr, ccs, ccr, rs, rr, gs, gr, ss, sr_sem, scs, scr,
):
    r, c = lax.axis_index("row"), lax.axis_index("col")
    zh, y = r // 4, r % 4
    chip, core = c // 2, c % 2
    oz, oc = 1 - zh, 1 - core
    ys = [(y + j) % 4 for j in (1, 2, 3)]
    chips = [(chip + j) % 8 for j in range(1, 8)]
    y_dev = [(zh * 4 + v, c) for v in ys]
    z_dev = (oz * 4 + y, c)
    chip_dev = [(r, v * 2 + core) for v in chips]
    core_dev = (r, chip * 2 + oc)

    def send(src, dst, ssem, rsem, dev):
        pltpu.make_async_remote_copy(
            src_ref=src, dst_ref=dst, send_sem=ssem, recv_sem=rsem, device_id=dev, device_id_type=MESH
        ).start()

    def await_bytes(like, sem):
        pltpu.make_async_copy(like, like, sem).wait()

    loads = [pltpu.make_async_copy(x_hbm.at[pl.ds(k * RB, RB)], xg.at[0, k, core, chip], lsem.at[k]) for k in range(K)]
    load_wi = pltpu.make_async_copy(wi_hbm, wi, lsem.at[K])
    load_wo = pltpu.make_async_copy(wo_hbm, wo, lsem.at[K + 1])
    load_t = pltpu.make_async_copy(t_hbm, tch, lsem.at[K + 2])
    for load in loads:
        load.start()

    barrier = pltpu.get_barrier_semaphore()
    peers = y_dev + [z_dev] + chip_dev + [core_dev]
    for peer in peers:
        pl.semaphore_signal(barrier, inc=1, device_id=peer, device_id_type=MESH)
    pl.semaphore_wait(barrier, len(peers))

    def gather_col_start(q, k):
        for dev in chip_dev:
            own = xg.at[q, k, core, chip]
            send(own, own, cs.at[q, k], cr.at[q, k], dev)

    def gather_col_mid(q, k):
        await_bytes(sr.at[q, k], cr.at[q, k])
        send(xg.at[q, k, core], xg.at[q, k, core], ccs.at[q, k], ccr.at[q, k], core_dev)

    def gather_col_end(q, k):
        await_bytes(sc.at[q, k], ccr.at[q, k])

    def product(out, left, right, transposed):
        depth = left.shape[-1]
        a = left[...].reshape(HALF, depth)
        if transposed:
            res = lax.dot_general(a, right[...], (((1,), (1,)), ((), ())), preferred_element_type=F32)
        else:
            res = jnp.dot(a, right[...], preferred_element_type=F32)
        out[...] = res.astype(BF16).reshape(out.shape)

    def row_start(q, k):
        weights, transposed = (wi, False) if q == 0 else (wo, True)
        product(hp.at[q, k, 1], xg.at[q, k, 1], weights, transposed)
        send(hp.at[q, k, 1, oz], hz.at[q, k], rs.at[q, k, 0], rr.at[q, k, 0], z_dev)
        product(hp.at[q, k, 0], xg.at[q, k, 0], weights, transposed)
        for j in (1, 0, 2):
            send(hp.at[q, k, 0, :, ys[j]], hy.at[q, k, j], rs.at[q, k, 1], rr.at[q, k, 1], y_dev[j])

    def row_mid(q, k):
        await_bytes(hz.at[q, k], rr.at[q, k, 0])
        hp[q, k, 1, zh] = (hp[q, k, 1, zh].astype(F32) + hz[q, k].astype(F32)).astype(BF16)
        for j in (1, 0, 2):
            send(hp.at[q, k, 1, zh, ys[j]], hy2.at[q, k, j], rs.at[q, k, 2], rr.at[q, k, 2], y_dev[j])
        await_bytes(hy.at[q, k], rr.at[q, k, 1])
        total = hp[q, k, 0, oz, y].astype(F32)
        for j in range(3):
            total = total + hy[q, k, j, oz].astype(F32)
        hp[q, k, 0, oz, y] = total.astype(BF16)
        send(hp.at[q, k, 0, oz, y], hz2.at[q, k], rs.at[q, k, 3], rr.at[q, k, 3], z_dev)

    def activate(q, k, part, total):
        if q == 0:
            hid[k, part] = total
            value = gelu_value(total)
        else:
            value = total * gelu_slope(hid[k, part])
        ag[q, k, part, zh, y] = value.astype(BF16)

    def row_end(q, k):
        await_bytes(hz2.at[q, k], rr.at[q, k, 3])
        total = hp[q, k, 0, zh, y].astype(F32) + hz2[q, k].astype(F32)
        for j in range(3):
            total = total + hy[q, k, j, zh].astype(F32)
        activate(q, k, 0, total)
        own = ag.at[q, k, 0, zh, y]
        send(own, own, gs.at[q, k, 0], gr.at[q, k, 0], z_dev)
        for j in (1, 0, 2):
            send(own, own, gs.at[q, k, 1], gr.at[q, k, 1], y_dev[j])
        await_bytes(hy2.at[q, k], rr.at[q, k, 2])
        total = hp[q, k, 1, zh, y].astype(F32)
        for j in range(3):
            total = total + hy2[q, k, j].astype(F32)
        activate(q, k, 1, total)
        own = ag.at[q, k, 1, zh, y]
        for j in (1, 0, 2):
            send(own, own, gs.at[q, k, 2], gr.at[q, k, 2], y_dev[j])
        send(own, own, gs.at[q, k, 3], gr.at[q, k, 3], z_dev)

    def gather_row_mid(q, k):
        await_bytes(hz2.at[q, k], gr.at[q, k, 0])
        for j in (1, 0, 2):
            got = ag.at[q, k, 0, oz, y]
            send(got, got, gs.at[q, k, 1], gr.at[q, k, 1], y_dev[j])
        await_bytes(hy2.at[q, k], gr.at[q, k, 2])
        for j in range(3):
            got = ag.at[q, k, 1, zh, ys[j]]
            send(got, got, gs.at[q, k, 3], gr.at[q, k, 3], z_dev)

    def col_start(q, k):
        await_bytes(hy.at[q, k], gr.at[q, k, 1])
        await_bytes(hz.at[q, k], gr.at[q, k, 3])
        weights, transposed = (wo, False) if q == 0 else (wi, True)
        product(sp.at[q, k, oc], ag.at[q, k, oc], weights, transposed)
        send(sp.at[q, k, oc], sc.at[q, k], scs.at[q, k], scr.at[q, k], core_dev)
        product(sp.at[q, k, core], ag.at[q, k, core], weights, transposed)

    def col_mid(q, k):
        await_bytes(sc.at[q, k], scr.at[q, k])
        sp[q, k, core] = (sp[q, k, core].astype(F32) + sc[q, k].astype(F32)).astype(BF16)
        for j, dev in enumerate(chip_dev):
            send(sp.at[q, k, core, chips[j]], sr.at[q, k, j], ss.at[q, k], sr_sem.at[q, k], dev)

    def col_end(q, k):
        await_bytes(sr.at[q, k], sr_sem.at[q, k])
        total = sp[q, k, core, chip].astype(F32)
        for j in range(7):
            total = total + sr[q, k, j].astype(F32)
        rows = pl.ds(k * RB, RB)
        if q == 0:
            xg[1, k, core, chip] = (0.125 * (total - tch[rows, :].astype(F32))).astype(BF16)
            gather_col_start(1, k)
        else:
            gi[rows, :] = total.astype(BF16)
            pltpu.make_async_copy(gi.at[rows], gi_hbm.at[rows], osem.at[2 + k]).start()

    def weight_grad(out, left, right, tile):
        b = right.reshape(K * 2 * HALF, right.shape[-1])
        a = left.reshape(K * 2 * HALF, left.shape[-1])

        def step(i, carry):
            at = pl.ds(pl.multiple_of(i * tile, tile), tile)
            out[at, :] = lax.dot_general(
                a[:, at], b[...], (((0,), (0,)), ((), ())), preferred_element_type=F32
            ).astype(BF16)
            return carry

        lax.fori_loop(0, out.shape[0] // tile, step, 0)

    for k in range(K):
        loads[k].wait()
        gather_col_start(0, k)
    load_wi.start()
    load_wo.start()
    load_t.start()

    for event in ORDER:
        k, e = ord(event[0]) - ord("A"), event[1:]
        if event == "G":
            weight_grad(gwo, ag.at[0], xg.at[1], 384)
            pltpu.make_async_copy(gwo, gwo_hbm, osem.at[1]).start()
        elif event == "W":
            weight_grad(gwi, xg.at[0], ag.at[1], 128)
            pltpu.make_async_copy(gwi, gwi_hbm, osem.at[0]).start()
        elif e == "0":
            gather_col_mid(0, k)
        elif e == "1":
            if k == 0:
                load_wi.wait()
            gather_col_end(0, k)
            row_start(0, k)
        elif e == "2":
            row_mid(0, k)
        elif e == "3":
            row_end(0, k)
        elif e == "4":
            gather_row_mid(0, k)
        elif e == "5":
            if k == 0:
                load_wo.wait()
                load_t.wait()
            col_start(0, k)
        elif e == "6":
            col_mid(0, k)
        elif e == "7":
            col_end(0, k)
        elif e == "8":
            gather_col_mid(1, k)
        elif e == "9":
            gather_col_end(1, k)
            row_start(1, k)
        elif e == "10":
            row_mid(1, k)
        elif e == "11":
            row_end(1, k)
        elif e == "12":
            gather_row_mid(1, k)
        elif e == "13":
            col_start(1, k)
        elif e == "14":
            col_mid(1, k)
        elif e == "15":
            col_end(1, k)

    for q in range(2):
        for k in range(K):
            await_bytes(sr.at[q, k], cs.at[q, k])
            await_bytes(sc.at[q, k], ccs.at[q, k])
            await_bytes(hz.at[q, k], rs.at[q, k, 0])
            await_bytes(hy.at[q, k], rs.at[q, k, 1])
            await_bytes(hy2.at[q, k], rs.at[q, k, 2])
            await_bytes(hz2.at[q, k], rs.at[q, k, 3])
            await_bytes(hz2.at[q, k], gs.at[q, k, 0])
            await_bytes(hy.at[q, k], gs.at[q, k, 1])
            await_bytes(hy2.at[q, k], gs.at[q, k, 2])
            await_bytes(hz.at[q, k], gs.at[q, k, 3])
            await_bytes(sc.at[q, k], scs.at[q, k])
            await_bytes(sr.at[q, k], ss.at[q, k])
    pltpu.make_async_copy(gwi, gwi_hbm, osem.at[0]).wait()
    pltpu.make_async_copy(gwo, gwo_hbm, osem.at[1]).wait()
    for k in range(K):
        rows = pl.ds(k * RB, RB)
        pltpu.make_async_copy(gi.at[rows], gi_hbm.at[rows], osem.at[2 + k]).wait()


def shards(inputs, teacher, weight_in, weight_out):
    tokens = inputs.shape[0]
    dma = lambda *shape: pltpu.SemaphoreType.DMA(shape)
    scratch = [
        pltpu.VMEM((D, H), BF16),
        pltpu.VMEM((H, D), BF16),
        pltpu.VMEM((tokens, D), BF16),
        pltpu.VMEM((tokens, D), BF16),
        pltpu.VMEM((D, H), BF16),
        pltpu.VMEM((H, D), BF16),
        pltpu.VMEM((K, 2, RB, H), F32),
        pltpu.VMEM((2, K, 2, 2, 4, RB, H), BF16),
        pltpu.VMEM((2, K, 4, RB, H), BF16),
        pltpu.VMEM((2, K, 3, 2, RB, H), BF16),
        pltpu.VMEM((2, K, RB, H), BF16),
        pltpu.VMEM((2, K, 3, RB, H), BF16),
        pltpu.VMEM((2, K, 2, 2, 4, RB, H), BF16),
        pltpu.VMEM((2, K, 2, 8, RB, D), BF16),
        pltpu.VMEM((2, K, 2, 8, RB, D), BF16),
        pltpu.VMEM((2, K, 8, RB, D), BF16),
        pltpu.VMEM((2, K, 7, RB, D), BF16),
        dma(K + 3), dma(2 + K),
        dma(2, K), dma(2, K), dma(2, K), dma(2, K),
        dma(2, K, 4), dma(2, K, 4), dma(2, K, 4), dma(2, K, 4),
        dma(2, K), dma(2, K), dma(2, K), dma(2, K),
    ]
    anywhere = pl.BlockSpec(memory_space=pl.ANY)
    return pl.pallas_call(
        kernel,
        out_shape=(
            jax.ShapeDtypeStruct((tokens, D), BF16),
            jax.ShapeDtypeStruct((D, H), BF16),
            jax.ShapeDtypeStruct((H, D), BF16),
        ),
        in_specs=[anywhere] * 4,
        out_specs=(anywhere,) * 3,
        scratch_shapes=scratch,
        compiler_params=pltpu.CompilerParams(
            collective_id=0, has_side_effects=True, vmem_limit_bytes=58 * 1024 * 1024
        ),
    )(inputs, teacher, weight_in, weight_out)


def solution(mesh):
    placed = (P("col", "row"), P("col", "row"), P("row", "col"), P("col", "row"))
    return jax.shard_map(
        shards,
        mesh=mesh,
        in_specs=placed,
        out_specs=(P("col", "row"), P("row", "col"), P("col", "row")),
        check_vma=False,
    )
```

time: 610 us -> 228 us (0.37)
  waiting for transfers between devices: 534 us -> 0 us
  Pallas kernels: 0 us -> 221 us
  matrix products: 48.9 us -> 0 us
  between operations: 14.2 us -> 0.64 us
  other arithmetic: 7.74 us -> 0 us
    reduce_scatter x4 -> x0, waiting for transfers between devices: 329 us -> none  [the longest x1 106 us: shards(): lax.psum_scatter(jnp.dot(block, weight_in, preferred_element_type=jnp.flo...]
    pallas_call x0 -> x1, Pallas kernels: none -> 221 us  [shards(): pl.pallas_call(kernel, out_shape=(jax.ShapeDtypeStruct((tokens, D), BF16)...]
    all_gather x4 -> x0, waiting for transfers between devices: 204 us -> none  [the longest x1 65.4 us: shards(): lax.all_gather(gelu_value(hidden).astype(jnp.bfloat16), 'row', axis=0, ti...]
    dot_general x6 -> x0, matrix products: 48.9 us -> none  [the longest x2 18.1 us: contract_cols(): lax.dot_general(left, right, (((1,), (1,)), ((), ())), preferred_element_...]
    convert_element_type x4 -> x0, other arithmetic: 7.74 us -> none  [the longest x1 2.29 us: shards(): (d_act * gelu_slope(hidden)).astype(jnp.bfloat16)]
  transfers between devices with their start and end apart: 8 -> 0, of which waited for: 8 -> 0; matrix products, arithmetic and copies ran while one was open for 3% -> 0% of each run, Pallas kernels for 0% -> 0%
where the time goes in v1:
time: 228 us
  Pallas kernels  221 us (97%)
  local copies, waits for them, and re-layouts  6.1 us (3%)
    pallas_call x1, Pallas kernels, shards(): pl.pallas_call(kernel, out_shape=(jax.ShapeDtypeStruct((tokens, D), BF16)...  221 us
    unnamed x5, local copies, waits for them, and re-layouts  6.1 us

profile of v1, /device:TPU:0, one launch (start us, length us, event | category | flops | bytes accessed | tf_op | source)
XLA Modules:
  0.0 227.5 jit_solution(8031711975135453534)
XLA Ops:
  0.6 220.8 %shard_map.67 = (bf16[96,896]{1,0:T(8,128)(2,1)}, bf16[896,1152]{1,0:T(8,128)(2,1)}, bf16[1152,896]{1,0:T(8,128)(2,1)}) custom-call(bf16[96,896]{1,0:T(8,128)(2,1)} %x_hbm.1, bf16[96,896]{1,0:T(8,128)(2,1)} %t_hbm.1, bf16[896,1152]{1,0:T(8,128)(2,1)} %wi_hbm.1, bf16[1152,896]{1,0:T(8,128)(2,1)} %wo_hbm.1), custom_call_target="tpu_custom_call" | custom-call | tf_op jit(solution)/shard_map/pallas_call | solution.py:297
  221.4 1.6 copy.10
  223.0 0.0 copy-start
  223.0 3.2 %copy.11 = bf16[896,1152]{1,0:T(8,128)(2,1)} copy(bf16[896,1152]{1,0:T(8,128)(2,1)} %get-tuple-element.7) | data formatting | bytes 4128768
  226.2 0.0 copy-done
  226.2 1.3 copy.12
Async XLA Ops:
  223.0 3.2 %copy-start = (bf16[1152,896]{1,0:T(8,128)(2,1)S(1)}, bf16[1152,896]{1,0:T(8,128)(2,1)}, u32[]{:S(2)}) copy-start(bf16[1152,896]{1,0:T(8,128)(2,1)} %get-tuple-element.8) | copy-start | bytes 6193156

commit v2 on v1

--- a/solution.py
+++ b/solution.py
@@ -11,17 +11,20 @@
 F32 = jnp.float32
 BF16 = jnp.bfloat16
 
-K = 2
+K = 3
 RB = 96 // K
 D = 896
 H = 1152
 HALF = 8 * RB
 
 ORDER = (
-    "A0", "B0", "A1", "B1", "A2", "B2", "A3", "B3", "A4", "A5",
-    "A6", "B4", "A7", "B5", "B6", "A8", "B7", "A9", "B8", "B9",
-    "A10", "G", "B10", "A11", "B11", "A12", "A13", "A14", "B12", "A15",
-    "B13", "W", "B14", "B15",
+    "A0gm", "A0gc", "B0gm", "C0gm", "A0rs", "B0gc", "C0gc", "B0rs", "A0rm", "A0re",
+    "B0rm", "C0rs", "A0am", "B0re", "C0rm", "A0cs", "B0am", "A0cm", "C0re", "A0cz",
+    "B0cs", "A0ce", "B0cm", "C0am", "C0cs", "A1gm", "B0cz", "B0ce", "A1gc", "C0cm",
+    "B1gm", "A1rs", "B1gc", "C0cz", "A1rm", "B1rs", "C0ce", "C1gm", "A1re", "C1gc",
+    "C1rs", "B1rm", "A1am", "B1re", "A1cs", "C1rm", "A1cm", "B1am", "C1re", "G",
+    "B1cs", "A1cz", "C1am", "B1cm", "C1cs", "B1cz", "C1cm", "B1ce", "W", "C1cz",
+    "A1ce", "C1ce",
 )
 
 
@@ -37,19 +40,20 @@
 def kernel(
     x_hbm, t_hbm, wi_hbm, wo_hbm, gi_hbm, gwi_hbm, gwo_hbm,
     wi, wo, tch, gi, gwi, gwo, hid,
-    hp, hz, hy, hz2, hy2, ag, xg, sp, sc, sr,
-    lsem, osem, cs, cr, ccs, ccr, rs, rr, gs, gr, ss, sr_sem, scs, scr,
+    hp, hz, hy, hz2, hy2, ag, xg, sp, sc, sx, sz,
+    lsem, osem, cs, cr, rs, rr, gs, gr, ss, st,
 ):
     r, c = lax.axis_index("row"), lax.axis_index("col")
     zh, y = r // 4, r % 4
-    chip, core = c // 2, c % 2
-    oz, oc = 1 - zh, 1 - core
+    zl, x, core = c // 8, c // 2 % 4, c % 2
+    oz, ol, oc = 1 - zh, 1 - zl, 1 - core
     ys = [(y + j) % 4 for j in (1, 2, 3)]
-    chips = [(chip + j) % 8 for j in range(1, 8)]
+    xs = [(x + j) % 4 for j in (1, 2, 3)]
     y_dev = [(zh * 4 + v, c) for v in ys]
     z_dev = (oz * 4 + y, c)
-    chip_dev = [(r, v * 2 + core) for v in chips]
-    core_dev = (r, chip * 2 + oc)
+    x_dev = [(r, zl * 8 + v * 2 + core) for v in xs]
+    l_dev = (r, ol * 8 + x * 2 + core)
+    core_dev = (r, zl * 8 + x * 2 + oc)
 
     def send(src, dst, ssem, rsem, dev):
         pltpu.make_async_remote_copy(
@@ -59,7 +63,7 @@
     def await_bytes(like, sem):
         pltpu.make_async_copy(like, like, sem).wait()
 
-    loads = [pltpu.make_async_copy(x_hbm.at[pl.ds(k * RB, RB)], xg.at[0, k, core, chip], lsem.at[k]) for k in range(K)]
+    loads = [pltpu.make_async_copy(x_hbm.at[pl.ds(k * RB, RB)], xg.at[0, k, core, zl, x], lsem.at[k]) for k in range(K)]
     load_wi = pltpu.make_async_copy(wi_hbm, wi, lsem.at[K])
     load_wo = pltpu.make_async_copy(wo_hbm, wo, lsem.at[K + 1])
     load_t = pltpu.make_async_copy(t_hbm, tch, lsem.at[K + 2])
@@ -67,22 +71,29 @@
         load.start()
 
     barrier = pltpu.get_barrier_semaphore()
-    peers = y_dev + [z_dev] + chip_dev + [core_dev]
+    peers = y_dev + x_dev + [z_dev, l_dev, core_dev]
     for peer in peers:
         pl.semaphore_signal(barrier, inc=1, device_id=peer, device_id_type=MESH)
     pl.semaphore_wait(barrier, len(peers))
 
     def gather_col_start(q, k):
-        for dev in chip_dev:
-            own = xg.at[q, k, core, chip]
-            send(own, own, cs.at[q, k], cr.at[q, k], dev)
+        own = xg.at[q, k, core, zl, x]
+        send(own, own, cs.at[q, k, 0], cr.at[q, k, 0], l_dev)
+        for j in (1, 0, 2):
+            send(own, own, cs.at[q, k, 1], cr.at[q, k, 1], x_dev[j])
 
     def gather_col_mid(q, k):
-        await_bytes(sr.at[q, k], cr.at[q, k])
-        send(xg.at[q, k, core], xg.at[q, k, core], ccs.at[q, k], ccr.at[q, k], core_dev)
+        await_bytes(sz.at[q, k], cr.at[q, k, 0])
+        for j in (1, 0, 2):
+            got = xg.at[q, k, core, ol, x]
+            send(got, got, cs.at[q, k, 1], cr.at[q, k, 1], x_dev[j])
+
+    def gather_col_core(q, k):
+        await_bytes(sx.at[q, k], cr.at[q, k, 1])
+        send(xg.at[q, k, core], xg.at[q, k, core], cs.at[q, k, 2], cr.at[q, k, 2], core_dev)
 
     def gather_col_end(q, k):
-        await_bytes(sc.at[q, k], ccr.at[q, k])
+        await_bytes(sc.at[q, k], cr.at[q, k, 2])
 
     def product(out, left, right, transposed):
         depth = left.shape[-1]
@@ -156,23 +167,31 @@
         await_bytes(hz.at[q, k], gr.at[q, k, 3])
         weights, transposed = (wo, False) if q == 0 else (wi, True)
         product(sp.at[q, k, oc], ag.at[q, k, oc], weights, transposed)
-        send(sp.at[q, k, oc], sc.at[q, k], scs.at[q, k], scr.at[q, k], core_dev)
+        send(sp.at[q, k, oc], sc.at[q, k], ss.at[q, k, 0], st.at[q, k, 0], core_dev)
         product(sp.at[q, k, core], ag.at[q, k, core], weights, transposed)
 
     def col_mid(q, k):
-        await_bytes(sc.at[q, k], scr.at[q, k])
+        await_bytes(sc.at[q, k], st.at[q, k, 0])
         sp[q, k, core] = (sp[q, k, core].astype(F32) + sc[q, k].astype(F32)).astype(BF16)
-        for j, dev in enumerate(chip_dev):
-            send(sp.at[q, k, core, chips[j]], sr.at[q, k, j], ss.at[q, k], sr_sem.at[q, k], dev)
+        for j in (1, 0, 2):
+            send(sp.at[q, k, core, :, xs[j]], sx.at[q, k, j], ss.at[q, k, 1], st.at[q, k, 1], x_dev[j])
+
+    def col_z(q, k):
+        await_bytes(sx.at[q, k], st.at[q, k, 1])
+        total = sp[q, k, core, ol, x].astype(F32)
+        for j in range(3):
+            total = total + sx[q, k, j, ol].astype(F32)
+        sp[q, k, core, ol, x] = total.astype(BF16)
+        send(sp.at[q, k, core, ol, x], sz.at[q, k], ss.at[q, k, 2], st.at[q, k, 2], l_dev)
 
     def col_end(q, k):
-        await_bytes(sr.at[q, k], sr_sem.at[q, k])
-        total = sp[q, k, core, chip].astype(F32)
-        for j in range(7):
-            total = total + sr[q, k, j].astype(F32)
+        await_bytes(sz.at[q, k], st.at[q, k, 2])
+        total = sp[q, k, core, zl, x].astype(F32) + sz[q, k].astype(F32)
+        for j in range(3):
+            total = total + sx[q, k, j, zl].astype(F32)
         rows = pl.ds(k * RB, RB)
         if q == 0:
-            xg[1, k, core, chip] = (0.125 * (total - tch[rows, :].astype(F32))).astype(BF16)
+            xg[1, k, core, zl, x] = (0.125 * (total - tch[rows, :].astype(F32))).astype(BF16)
             gather_col_start(1, k)
         else:
             gi[rows, :] = total.astype(BF16)
@@ -198,58 +217,38 @@
     load_wo.start()
     load_t.start()
 
+    steps = {
+        "gm": gather_col_mid, "gc": gather_col_core, "rm": row_mid, "re": row_end,
+        "am": gather_row_mid, "cm": col_mid, "cz": col_z, "ce": col_end,
+    }
     for event in ORDER:
-        k, e = ord(event[0]) - ord("A"), event[1:]
         if event == "G":
             weight_grad(gwo, ag.at[0], xg.at[1], 384)
             pltpu.make_async_copy(gwo, gwo_hbm, osem.at[1]).start()
-        elif event == "W":
+            continue
+        if event == "W":
             weight_grad(gwi, xg.at[0], ag.at[1], 128)
             pltpu.make_async_copy(gwi, gwi_hbm, osem.at[0]).start()
-        elif e == "0":
-            gather_col_mid(0, k)
-        elif e == "1":
-            if k == 0:
+            continue
+        k, q, step = ord(event[0]) - ord("A"), int(event[1]), event[2:]
+        if step == "rs":
+            if event == "A0rs":
                 load_wi.wait()
-            gather_col_end(0, k)
-            row_start(0, k)
-        elif e == "2":
-            row_mid(0, k)
-        elif e == "3":
-            row_end(0, k)
-        elif e == "4":
-            gather_row_mid(0, k)
-        elif e == "5":
-            if k == 0:
+            gather_col_end(q, k)
+            row_start(q, k)
+        elif step == "cs":
+            if event == "A0cs":
                 load_wo.wait()
                 load_t.wait()
-            col_start(0, k)
-        elif e == "6":
-            col_mid(0, k)
-        elif e == "7":
-            col_end(0, k)
-        elif e == "8":
-            gather_col_mid(1, k)
-        elif e == "9":
-            gather_col_end(1, k)
-            row_start(1, k)
-        elif e == "10":
-            row_mid(1, k)
-        elif e == "11":
-            row_end(1, k)
-        elif e == "12":
-            gather_row_mid(1, k)
-        elif e == "13":
-            col_start(1, k)
-        elif e == "14":
-            col_mid(1, k)
-        elif e == "15":
-            col_end(1, k)
+            col_start(q, k)
+        else:
+            steps[step](q, k)
 
     for q in range(2):
         for k in range(K):
-            await_bytes(sr.at[q, k], cs.at[q, k])
-            await_bytes(sc.at[q, k], ccs.at[q, k])
+            await_bytes(sz.at[q, k], cs.at[q, k, 0])
+            await_bytes(sx.at[q, k], cs.at[q, k, 1])
+            await_bytes(sc.at[q, k], cs.at[q, k, 2])
             await_bytes(hz.at[q, k], rs.at[q, k, 0])
             await_bytes(hy.at[q, k], rs.at[q, k, 1])
             await_bytes(hy2.at[q, k], rs.at[q, k, 2])
@@ -258,8 +257,9 @@
             await_bytes(hy.at[q, k], gs.at[q, k, 1])
             await_bytes(hy2.at[q, k], gs.at[q, k, 2])
             await_bytes(hz.at[q, k], gs.at[q, k, 3])
-            await_bytes(sc.at[q, k], scs.at[q, k])
-            await_bytes(sr.at[q, k], ss.at[q, k])
+            await_bytes(sc.at[q, k], ss.at[q, k, 0])
+            await_bytes(sx.at[q, k], ss.at[q, k, 1])
+            await_bytes(sz.at[q, k], ss.at[q, k, 2])
     pltpu.make_async_copy(gwi, gwi_hbm, osem.at[0]).wait()
     pltpu.make_async_copy(gwo, gwo_hbm, osem.at[1]).wait()
     for k in range(K):
@@ -284,14 +284,14 @@
         pltpu.VMEM((2, K, RB, H), BF16),
         pltpu.VMEM((2, K, 3, RB, H), BF16),
         pltpu.VMEM((2, K, 2, 2, 4, RB, H), BF16),
-        pltpu.VMEM((2, K, 2, 8, RB, D), BF16),
-        pltpu.VMEM((2, K, 2, 8, RB, D), BF16),
-        pltpu.VMEM((2, K, 8, RB, D), BF16),
-        pltpu.VMEM((2, K, 7, RB, D), BF16),
+        pltpu.VMEM((2, K, 2, 2, 4, RB, D), BF16),
+        pltpu.VMEM((2, K, 2, 2, 4, RB, D), BF16),
+        pltpu.VMEM((2, K, 2, 4, RB, D), BF16),
+        pltpu.VMEM((2, K, 3, 2, RB, D), BF16),
+        pltpu.VMEM((2, K, RB, D), BF16),
         dma(K + 3), dma(2 + K),
-        dma(2, K), dma(2, K), dma(2, K), dma(2, K),
-        dma(2, K, 4), dma(2, K, 4), dma(2, K, 4), dma(2, K, 4),
-        dma(2, K), dma(2, K), dma(2, K), dma(2, K),
+        dma(2, K, 3), dma(2, K, 3), dma(2, K, 4), dma(2, K, 4),
+        dma(2, K, 4), dma(2, K, 4), dma(2, K, 3), dma(2, K, 3),
     ]
     anywhere = pl.BlockSpec(memory_space=pl.ANY)
     return pl.pallas_call(

time: 228 us -> 186 us (0.82)
  Pallas kernels: 221 us -> 180 us
    pallas_call x1, Pallas kernels: 221 us -> 180 us  [shards(): pl.pallas_call(kernel, out_shape=(jax.ShapeDtypeStruct((tokens, D), BF16)...]
where the time goes in v2:
time: 186 us
  Pallas kernels  180 us (97%)
  local copies, waits for them, and re-layouts  6.1 us (3%)
    pallas_call x1, Pallas kernels, shards(): pl.pallas_call(kernel, out_shape=(jax.ShapeDtypeStruct((tokens, D), BF16)...  180 us
    unnamed x5, local copies, waits for them, and re-layouts  6.1 us

profile of v2, /device:TPU:0, one launch (start us, length us, event | category | flops | bytes accessed | tf_op | source)
XLA Modules:
  0.0 186.3 jit_solution(2646016905707482225)
XLA Ops:
  0.6 179.6 %shard_map.67 = (bf16[96,896]{1,0:T(8,128)(2,1)}, bf16[896,1152]{1,0:T(8,128)(2,1)}, bf16[1152,896]{1,0:T(8,128)(2,1)}) custom-call(bf16[96,896]{1,0:T(8,128)(2,1)} %x_hbm.1, bf16[96,896]{1,0:T(8,128)(2,1)} %t_hbm.1, bf16[896,1152]{1,0:T(8,128)(2,1)} %wi_hbm.1, bf16[1152,896]{1,0:T(8,128)(2,1)} %wo_hbm.1), custom_call_target="tpu_custom_call" | custom-call | tf_op jit(solution)/shard_map/pallas_call | solution.py:297
  180.2 1.6 copy.10
  181.8 0.0 copy-start
  181.8 3.2 %copy.11 = bf16[896,1152]{1,0:T(8,128)(2,1)} copy(bf16[896,1152]{1,0:T(8,128)(2,1)} %get-tuple-element.7) | data formatting | bytes 4128768
  185.0 0.0 copy-done
  185.0 1.3 copy.12
Async XLA Ops:
  181.8 3.2 %copy-start = (bf16[1152,896]{1,0:T(8,128)(2,1)S(1)}, bf16[1152,896]{1,0:T(8,128)(2,1)}, u32[]{:S(2)}) copy-start(bf16[1152,896]{1,0:T(8,128)(2,1)} %get-tuple-element.8) | copy-start | bytes 6193156

commit v3 on v2

--- a/solution.py
+++ b/solution.py
@@ -11,20 +11,29 @@
 F32 = jnp.float32
 BF16 = jnp.bfloat16
 
-K = 3
+K = 6
 RB = 96 // K
 D = 896
 H = 1152
 HALF = 8 * RB
 
 ORDER = (
-    "A0gm", "A0gc", "B0gm", "C0gm", "A0rs", "B0gc", "C0gc", "B0rs", "A0rm", "A0re",
-    "B0rm", "C0rs", "A0am", "B0re", "C0rm", "A0cs", "B0am", "A0cm", "C0re", "A0cz",
-    "B0cs", "A0ce", "B0cm", "C0am", "C0cs", "A1gm", "B0cz", "B0ce", "A1gc", "C0cm",
-    "B1gm", "A1rs", "B1gc", "C0cz", "A1rm", "B1rs", "C0ce", "C1gm", "A1re", "C1gc",
-    "C1rs", "B1rm", "A1am", "B1re", "A1cs", "C1rm", "A1cm", "B1am", "C1re", "G",
-    "B1cs", "A1cz", "C1am", "B1cm", "C1cs", "B1cz", "C1cm", "B1ce", "W", "C1cz",
-    "A1ce", "C1ce",
+    "A0gm", "A0gc", "B0gm", "A0rs", "B0gc", "F0gm", "C0gm", "B0rs", "C0gc", "A0rB",
+    "A0rC", "D0gm", "A0rE", "A0rF", "B0rB", "A0aA", "D0gc", "B0rC", "C0rs", "C0rC",
+    "A0aD", "F0gc", "B0rE", "C0rB", "E0gm", "D0rs", "B0rF", "E0gc", "A0cs", "C0rF",
+    "C0rE", "B0aD", "D0rB", "B0aA", "E0rs", "A0cm", "A0cz", "D0rC", "B0cs", "E0rB",
+    "D0rE", "A0ce", "D0rF", "C0aA", "B0cm", "C0aD", "A1gm", "F0rs", "B0cz", "C0cs",
+    "D0aA", "D0aD", "E0rC", "F0rB", "C0cm", "E0rE", "A1gc", "B0ce", "F0rC", "E0rF",
+    "A1rs", "B1gm", "D0cs", "F0rE", "D0cm", "E0aA", "C0cz", "B1gc", "E0aD", "C0ce",
+    "F0rF", "A1rC", "D0cz", "A1rB", "B1rs", "F0aA", "E0cs", "A1rE", "C1gm", "F0aD",
+    "E0cm", "C1gc", "A1aA", "D0ce", "F0cs", "B1rB", "E0cz", "B1rC", "A1rF", "C1rs",
+    "D1gm", "F0cm", "D1gc", "B1rE", "E0ce", "F0cz", "A1aD", "C1rC", "E1gm", "D1rs",
+    "B1rF", "E1gc", "C1rB", "A1cs", "B1aA", "C1rF", "F0ce", "B1aD", "A1cm", "D1rB",
+    "D1rC", "C1rE", "F1gm", "E1rs", "F1gc", "D1rF", "B1cs", "C1aA", "D1rE", "A1cz",
+    "C1aD", "F1rs", "E1rC", "B1cm", "G", "D1aA", "B1cz", "E1rB", "D1aD", "E1rF",
+    "C1cs", "E1rE", "F1rB", "B1ce", "A1ce", "F1rC", "C1cm", "E1aA", "E1aD", "D1cs",
+    "F1rE", "F1rF", "E1cs", "D1cm", "F1aD", "F1aA", "E1cm", "D1cz", "F1cs", "C1cz",
+    "E1cz", "F1cm", "W", "F1cz", "E1ce", "C1ce", "D1ce", "F1ce",
 )
 
 
@@ -96,8 +105,7 @@
         await_bytes(sc.at[q, k], cr.at[q, k, 2])
 
     def product(out, left, right, transposed):
-        depth = left.shape[-1]
-        a = left[...].reshape(HALF, depth)
+        a = left[...].reshape(2 * HALF, left.shape[-1])
         if transposed:
             res = lax.dot_general(a, right[...], (((1,), (1,)), ((), ())), preferred_element_type=F32)
         else:
@@ -105,18 +113,20 @@
         out[...] = res.astype(BF16).reshape(out.shape)
 
     def row_start(q, k):
+        gather_col_end(q, k)
         weights, transposed = (wi, False) if q == 0 else (wo, True)
-        product(hp.at[q, k, 1], xg.at[q, k, 1], weights, transposed)
+        product(hp.at[q, k], xg.at[q, k], weights, transposed)
         send(hp.at[q, k, 1, oz], hz.at[q, k], rs.at[q, k, 0], rr.at[q, k, 0], z_dev)
-        product(hp.at[q, k, 0], xg.at[q, k, 0], weights, transposed)
         for j in (1, 0, 2):
             send(hp.at[q, k, 0, :, ys[j]], hy.at[q, k, j], rs.at[q, k, 1], rr.at[q, k, 1], y_dev[j])
 
-    def row_mid(q, k):
+    def row_after_z(q, k):
         await_bytes(hz.at[q, k], rr.at[q, k, 0])
         hp[q, k, 1, zh] = (hp[q, k, 1, zh].astype(F32) + hz[q, k].astype(F32)).astype(BF16)
         for j in (1, 0, 2):
             send(hp.at[q, k, 1, zh, ys[j]], hy2.at[q, k, j], rs.at[q, k, 2], rr.at[q, k, 2], y_dev[j])
+
+    def row_after_y(q, k):
         await_bytes(hy.at[q, k], rr.at[q, k, 1])
         total = hp[q, k, 0, oz, y].astype(F32)
         for j in range(3):
@@ -132,7 +142,7 @@
             value = total * gelu_slope(hid[k, part])
         ag[q, k, part, zh, y] = value.astype(BF16)
 
-    def row_end(q, k):
+    def row_end_z(q, k):
         await_bytes(hz2.at[q, k], rr.at[q, k, 3])
         total = hp[q, k, 0, zh, y].astype(F32) + hz2[q, k].astype(F32)
         for j in range(3):
@@ -142,6 +152,8 @@
         send(own, own, gs.at[q, k, 0], gr.at[q, k, 0], z_dev)
         for j in (1, 0, 2):
             send(own, own, gs.at[q, k, 1], gr.at[q, k, 1], y_dev[j])
+
+    def row_end_y(q, k):
         await_bytes(hy2.at[q, k], rr.at[q, k, 2])
         total = hp[q, k, 1, zh, y].astype(F32)
         for j in range(3):
@@ -152,11 +164,13 @@
             send(own, own, gs.at[q, k, 2], gr.at[q, k, 2], y_dev[j])
         send(own, own, gs.at[q, k, 3], gr.at[q, k, 3], z_dev)
 
-    def gather_row_mid(q, k):
+    def gather_row_z(q, k):
         await_bytes(hz2.at[q, k], gr.at[q, k, 0])
         for j in (1, 0, 2):
             got = ag.at[q, k, 0, oz, y]
             send(got, got, gs.at[q, k, 1], gr.at[q, k, 1], y_dev[j])
+
+    def gather_row_y(q, k):
         await_bytes(hy2.at[q, k], gr.at[q, k, 2])
         for j in range(3):
             got = ag.at[q, k, 1, zh, ys[j]]
@@ -166,9 +180,8 @@
         await_bytes(hy.at[q, k], gr.at[q, k, 1])
         await_bytes(hz.at[q, k], gr.at[q, k, 3])
         weights, transposed = (wo, False) if q == 0 else (wi, True)
-        product(sp.at[q, k, oc], ag.at[q, k, oc], weights, transposed)
+        product(sp.at[q, k], ag.at[q, k], weights, transposed)
         send(sp.at[q, k, oc], sc.at[q, k], ss.at[q, k, 0], st.at[q, k, 0], core_dev)
-        product(sp.at[q, k, core], ag.at[q, k, core], weights, transposed)
 
     def col_mid(q, k):
         await_bytes(sc.at[q, k], st.at[q, k, 0])
@@ -218,30 +231,22 @@
     load_t.start()
 
     steps = {
-        "gm": gather_col_mid, "gc": gather_col_core, "rm": row_mid, "re": row_end,
-        "am": gather_row_mid, "cm": col_mid, "cz": col_z, "ce": col_end,
+        "gm": gather_col_mid, "gc": gather_col_core, "rs": row_start, "rC": row_after_z, "rB": row_after_y,
+        "rE": row_end_z, "rF": row_end_y, "aA": gather_row_z, "aD": gather_row_y,
+        "cs": col_start, "cm": col_mid, "cz": col_z, "ce": col_end,
     }
+    first = {"rs": [load_wi], "cs": [load_wo, load_t]}
     for event in ORDER:
         if event == "G":
             weight_grad(gwo, ag.at[0], xg.at[1], 384)
             pltpu.make_async_copy(gwo, gwo_hbm, osem.at[1]).start()
-            continue
-        if event == "W":
+        elif event == "W":
             weight_grad(gwi, xg.at[0], ag.at[1], 128)
             pltpu.make_async_copy(gwi, gwi_hbm, osem.at[0]).start()
-            continue
-        k, q, step = ord(event[0]) - ord("A"), int(event[1]), event[2:]
-        if step == "rs":
-            if event == "A0rs":
-                load_wi.wait()
-            gather_col_end(q, k)
-            row_start(q, k)
-        elif step == "cs":
-            if event == "A0cs":
-                load_wo.wait()
-                load_t.wait()
-            col_start(q, k)
         else:
+            k, q, step = ord(event[0]) - ord("A"), int(event[1]), event[2:]
+            for load in first.pop(step, []):
+                load.wait()
             steps[step](q, k)
 
     for q in range(2):

time: 186 us -> 167 us (0.90)
  Pallas kernels: 180 us -> 159 us
    pallas_call x1, Pallas kernels: 180 us -> 159 us  [shards(): pl.pallas_call(kernel, out_shape=(jax.ShapeDtypeStruct((tokens, D), BF16)...]
where the time goes in v3:
time: 167 us; the launch traced here: 166 us
  Pallas kernels  159 us (95%)
  local copies, waits for them, and re-layouts  6.1 us (4%)
    pallas_call x1, Pallas kernels, shards(): pl.pallas_call(kernel, out_shape=(jax.ShapeDtypeStruct((tokens, D), BF16)...  159 us
    unnamed x5, local copies, waits for them, and re-layouts  6.1 us

profile of v3, /device:TPU:0, one launch (start us, length us, event | category | flops | bytes accessed | tf_op | source)
XLA Modules:
  0.0 165.6 jit_solution(16119043713366258855)
XLA Ops:
  0.6 158.8 %shard_map.67 = (bf16[96,896]{1,0:T(8,128)(2,1)}, bf16[896,1152]{1,0:T(8,128)(2,1)}, bf16[1152,896]{1,0:T(8,128)(2,1)}) custom-call(bf16[96,896]{1,0:T(8,128)(2,1)} %x_hbm.1, bf16[96,896]{1,0:T(8,128)(2,1)} %t_hbm.1, bf16[896,1152]{1,0:T(8,128)(2,1)} %wi_hbm.1, bf16[1152,896]{1,0:T(8,128)(2,1)} %wo_hbm.1), custom_call_target="tpu_custom_call" | custom-call | tf_op jit(solution)/shard_map/pallas_call | solution.py:302
  159.5 1.6 copy.10
  161.1 0.0 copy-start
  161.1 3.2 %copy.11 = bf16[896,1152]{1,0:T(8,128)(2,1)} copy(bf16[896,1152]{1,0:T(8,128)(2,1)} %get-tuple-element.7) | data formatting | bytes 4128768
  164.3 0.0 copy-done
  164.3 1.3 copy.12
Async XLA Ops:
  161.1 3.2 %copy-start = (bf16[1152,896]{1,0:T(8,128)(2,1)S(1)}, bf16[1152,896]{1,0:T(8,128)(2,1)}, u32[]{:S(2)}) copy-start(bf16[1152,896]{1,0:T(8,128)(2,1)} %get-tuple-element.8) | copy-start | bytes 6193156

commit v4 on v3

--- a/solution.py
+++ b/solution.py
@@ -16,24 +16,27 @@
 D = 896
 H = 1152
 HALF = 8 * RB
+CZ = 640
+CY = H - CZ
 
 ORDER = (
-    "A0gm", "A0gc", "B0gm", "A0rs", "B0gc", "F0gm", "C0gm", "B0rs", "C0gc", "A0rB",
-    "A0rC", "D0gm", "A0rE", "A0rF", "B0rB", "A0aA", "D0gc", "B0rC", "C0rs", "C0rC",
-    "A0aD", "F0gc", "B0rE", "C0rB", "E0gm", "D0rs", "B0rF", "E0gc", "A0cs", "C0rF",
-    "C0rE", "B0aD", "D0rB", "B0aA", "E0rs", "A0cm", "A0cz", "D0rC", "B0cs", "E0rB",
-    "D0rE", "A0ce", "D0rF", "C0aA", "B0cm", "C0aD", "A1gm", "F0rs", "B0cz", "C0cs",
-    "D0aA", "D0aD", "E0rC", "F0rB", "C0cm", "E0rE", "A1gc", "B0ce", "F0rC", "E0rF",
-    "A1rs", "B1gm", "D0cs", "F0rE", "D0cm", "E0aA", "C0cz", "B1gc", "E0aD", "C0ce",
-    "F0rF", "A1rC", "D0cz", "A1rB", "B1rs", "F0aA", "E0cs", "A1rE", "C1gm", "F0aD",
-    "E0cm", "C1gc", "A1aA", "D0ce", "F0cs", "B1rB", "E0cz", "B1rC", "A1rF", "C1rs",
-    "D1gm", "F0cm", "D1gc", "B1rE", "E0ce", "F0cz", "A1aD", "C1rC", "E1gm", "D1rs",
-    "B1rF", "E1gc", "C1rB", "A1cs", "B1aA", "C1rF", "F0ce", "B1aD", "A1cm", "D1rB",
-    "D1rC", "C1rE", "F1gm", "E1rs", "F1gc", "D1rF", "B1cs", "C1aA", "D1rE", "A1cz",
-    "C1aD", "F1rs", "E1rC", "B1cm", "G", "D1aA", "B1cz", "E1rB", "D1aD", "E1rF",
-    "C1cs", "E1rE", "F1rB", "B1ce", "A1ce", "F1rC", "C1cm", "E1aA", "E1aD", "D1cs",
-    "F1rE", "F1rF", "E1cs", "D1cm", "F1aD", "F1aA", "E1cm", "D1cz", "F1cs", "C1cz",
-    "E1cz", "F1cm", "W", "F1cz", "E1ce", "C1ce", "D1ce", "F1ce",
+    "A0gm", "A0gc", "E0gm", "D0gm", "A0rs", "C0gm", "E0gc", "D0gc", "A0rA", "B0gm",
+    "C0gc", "E0rs", "A0rC", "A0rB", "C0rs", "D0rs", "A0rF", "E0rA", "E0rC", "F0gm",
+    "B0gc", "B0rs", "D0rA", "A0rE", "A0aD", "D0rC", "B0rA", "C0rA", "B0rC", "D0rB",
+    "A0aB", "D0rF", "F0gc", "B0rB", "D0rE", "F0rs", "B0rF", "E0rB", "B0rE", "A0cs",
+    "D0aD", "F0rA", "D0aB", "B0aD", "A0cm", "E0rF", "E0rE", "B0aB", "D0cs", "C0rB",
+    "C0rC", "A0cz", "E0aD", "D0cm", "F0rC", "B0cs", "F0rB", "E0aB", "A0ce", "C0rF",
+    "B0cm", "D0cz", "C0rE", "E0cs", "F0rF", "A1gm", "C0aD", "D0ce", "F0rE", "B0cz",
+    "E0cm", "A1gc", "F0aD", "C0aB", "D1gm", "B0ce", "F0aB", "E0cz", "C0cs", "A1rs",
+    "B1gm", "D1gc", "E0ce", "C0cm", "F0cs", "B1gc", "D1rs", "F0cm", "A1rA", "B1rs",
+    "C0cz", "E1gm", "D1rC", "A1rC", "B1rA", "F0cz", "E1gc", "A1rB", "C0ce", "B1rC",
+    "F0ce", "E1rs", "C1gm", "A1rE", "A1rF", "F1gm", "B1rB", "C1gc", "B1rF", "E1rA",
+    "F1gc", "C1rs", "F1rs", "B1rE", "E1rC", "D1rA", "E1rB", "G", "C1rA", "B1aD",
+    "C1rC", "D1rB", "E1rF", "A1aB", "C1rB", "D1rF", "A1aD", "F1rA", "E1rE", "D1rE",
+    "D1aD", "B1aB", "C1rF", "A1cs", "F1rB", "F1rC", "D1aB", "E1aD", "A1cm", "C1rE",
+    "E1aB", "B1cs", "C1aD", "F1rF", "D1cs", "F1rE", "B1cm", "A1cz", "E1cs", "D1cm",
+    "C1aB", "F1aD", "F1aB", "E1cm", "C1cs", "B1cz", "F1cs", "D1cz", "C1cm", "A1ce",
+    "E1cz", "B1ce", "F1cm", "W", "C1cz", "D1ce", "F1cz", "C1ce", "E1ce", "F1ce",
 )
 
 
@@ -48,8 +51,8 @@
 
 def kernel(
     x_hbm, t_hbm, wi_hbm, wo_hbm, gi_hbm, gwi_hbm, gwo_hbm,
-    wi, wo, tch, gi, gwi, gwo, hid,
-    hp, hz, hy, hz2, hy2, ag, xg, sp, sc, sx, sz,
+    wi, wo, tch, gi, gwi, gwo, hid_z, hid_y,
+    hp, hz, hr, hy, hz2, hy2, ag, xg, sp, sc, sx, sz,
     lsem, osem, cs, cr, rs, rr, gs, gr, ss, st,
 ):
     r, c = lax.axis_index("row"), lax.axis_index("col")
@@ -59,6 +62,9 @@
     ys = [(y + j) % 4 for j in (1, 2, 3)]
     xs = [(x + j) % 4 for j in (1, 2, 3)]
     y_dev = [(zh * 4 + v, c) for v in ys]
+    up, across, down = ys
+    up_dev, down_dev = y_dev[0], y_dev[2]
+    fz, fy = pl.ds(0, CZ), pl.ds(CZ, CY)
     z_dev = (oz * 4 + y, c)
     x_dev = [(r, zl * 8 + v * 2 + core) for v in xs]
     l_dev = (r, ol * 8 + x * 2 + core)
@@ -116,68 +122,77 @@
         gather_col_end(q, k)
         weights, transposed = (wi, False) if q == 0 else (wo, True)
         product(hp.at[q, k], xg.at[q, k], weights, transposed)
-        send(hp.at[q, k, 1, oz], hz.at[q, k], rs.at[q, k, 0], rr.at[q, k, 0], z_dev)
-        for j in (1, 0, 2):
-            send(hp.at[q, k, 0, :, ys[j]], hy.at[q, k, j], rs.at[q, k, 1], rr.at[q, k, 1], y_dev[j])
-
-    def row_after_z(q, k):
-        await_bytes(hz.at[q, k], rr.at[q, k, 0])
-        hp[q, k, 1, zh] = (hp[q, k, 1, zh].astype(F32) + hz[q, k].astype(F32)).astype(BF16)
-        for j in (1, 0, 2):
-            send(hp.at[q, k, 1, zh, ys[j]], hy2.at[q, k, j], rs.at[q, k, 2], rr.at[q, k, 2], y_dev[j])
+        part = hp.at[q, k]
+        send(part.at[:, 0, across, :, fz], hr.at[q, k, 0], rs.at[q, k, 0], rr.at[q, k, 0], up_dev)
+        send(part.at[:, 1, across, :, fz], hr.at[q, k, 1], rs.at[q, k, 0], rr.at[q, k, 0], down_dev)
+        send(part.at[:, oz, :, :, fy], hz.at[q, k], rs.at[q, k, 3], rr.at[q, k, 3], z_dev)
+        send(part.at[:, 1, up, :, fz], hy.at[q, k, 0, 1], rs.at[q, k, 1], rr.at[q, k, 1], up_dev)
+        send(part.at[:, 0, down, :, fz], hy.at[q, k, 1, 0], rs.at[q, k, 1], rr.at[q, k, 1], down_dev)
+
+    def row_relay(q, k):
+        await_bytes(hr.at[q, k], rr.at[q, k, 0])
+        for a, to, dev in ((0, up, up_dev), (1, down, down_dev)):
+            total = hp[q, k, :, a, to, :, fz].astype(F32) + hr[q, k, a].astype(F32)
+            hp[q, k, :, a, to, :, fz] = total.astype(BF16)
+            send(hp.at[q, k, :, a, to, :, fz], hy.at[q, k, a, a], rs.at[q, k, 1], rr.at[q, k, 1], dev)
 
     def row_after_y(q, k):
         await_bytes(hy.at[q, k], rr.at[q, k, 1])
-        total = hp[q, k, 0, oz, y].astype(F32)
-        for j in range(3):
-            total = total + hy[q, k, j, oz].astype(F32)
-        hp[q, k, 0, oz, y] = total.astype(BF16)
-        send(hp.at[q, k, 0, oz, y], hz2.at[q, k], rs.at[q, k, 3], rr.at[q, k, 3], z_dev)
-
-    def activate(q, k, part, total):
+        for b in range(2):
+            total = hp[q, k, :, b, y, :, fz].astype(F32)
+            total = total + hy[q, k, 0, b].astype(F32) + hy[q, k, 1, b].astype(F32)
+            hp[q, k, :, b, y, :, fz] = total.astype(BF16)
+        send(hp.at[q, k, :, :, y, :, fz], hz2.at[q, k], rs.at[q, k, 2], rr.at[q, k, 2], z_dev)
+
+    def row_after_z(q, k):
+        await_bytes(hz.at[q, k], rr.at[q, k, 3])
+        hp[q, k, :, zh, :, :, fy] = (hp[q, k, :, zh, :, :, fy].astype(F32) + hz[q, k].astype(F32)).astype(BF16)
+        for j in (1, 0, 2):
+            send(hp.at[q, k, :, zh, ys[j], :, fy], hy2.at[q, k, j], rs.at[q, k, 4], rr.at[q, k, 4], y_dev[j])
+
+    def row_end_z(q, k):
+        await_bytes(hz2.at[q, k], rr.at[q, k, 2])
+        total = hp[q, k, :, :, y, :, fz].astype(F32) + hz2[q, k].astype(F32)
         if q == 0:
-            hid[k, part] = total
+            hid_z[k] = total
             value = gelu_value(total)
         else:
-            value = total * gelu_slope(hid[k, part])
-        ag[q, k, part, zh, y] = value.astype(BF16)
-
-    def row_end_z(q, k):
-        await_bytes(hz2.at[q, k], rr.at[q, k, 3])
-        total = hp[q, k, 0, zh, y].astype(F32) + hz2[q, k].astype(F32)
-        for j in range(3):
-            total = total + hy[q, k, j, zh].astype(F32)
-        activate(q, k, 0, total)
-        own = ag.at[q, k, 0, zh, y]
-        send(own, own, gs.at[q, k, 0], gr.at[q, k, 0], z_dev)
-        for j in (1, 0, 2):
-            send(own, own, gs.at[q, k, 1], gr.at[q, k, 1], y_dev[j])
+            value = total * gelu_slope(hid_z[k])
+        ag[q, k, :, :, y, :, fz] = value.astype(BF16)
+        own = ag.at[q, k, :, :, y, :, fz]
+        for dev in (up_dev, down_dev):
+            send(own, own, gs.at[q, k, 0], gr.at[q, k, 0], dev)
 
     def row_end_y(q, k):
-        await_bytes(hy2.at[q, k], rr.at[q, k, 2])
-        total = hp[q, k, 1, zh, y].astype(F32)
+        await_bytes(hy2.at[q, k], rr.at[q, k, 4])
+        total = hp[q, k, :, zh, y, :, fy].astype(F32)
         for j in range(3):
             total = total + hy2[q, k, j].astype(F32)
-        activate(q, k, 1, total)
-        own = ag.at[q, k, 1, zh, y]
+        if q == 0:
+            hid_y[k] = total
+            value = gelu_value(total)
+        else:
+            value = total * gelu_slope(hid_y[k])
+        ag[q, k, :, zh, y, :, fy] = value.astype(BF16)
+        own = ag.at[q, k, :, zh, y, :, fy]
         for j in (1, 0, 2):
             send(own, own, gs.at[q, k, 2], gr.at[q, k, 2], y_dev[j])
         send(own, own, gs.at[q, k, 3], gr.at[q, k, 3], z_dev)
 
-    def gather_row_z(q, k):
-        await_bytes(hz2.at[q, k], gr.at[q, k, 0])
-        for j in (1, 0, 2):
-            got = ag.at[q, k, 0, oz, y]
-            send(got, got, gs.at[q, k, 1], gr.at[q, k, 1], y_dev[j])
+    def gather_row_relay(q, k):
+        await_bytes(hy.at[q, k], gr.at[q, k, 0])
+        for a, src, dev in ((0, down, up_dev), (1, up, down_dev)):
+            got = ag.at[q, k, :, a, src, :, fz]
+            send(got, got, gs.at[q, k, 1], gr.at[q, k, 1], dev)
 
     def gather_row_y(q, k):
         await_bytes(hy2.at[q, k], gr.at[q, k, 2])
         for j in range(3):
-            got = ag.at[q, k, 1, zh, ys[j]]
+            got = ag.at[q, k, :, zh, ys[j], :, fy]
             send(got, got, gs.at[q, k, 3], gr.at[q, k, 3], z_dev)
 
     def col_start(q, k):
-        await_bytes(hy.at[q, k], gr.at[q, k, 1])
+        await_bytes(hr.at[q, k], gr.at[q, k, 1])
         await_bytes(hz.at[q, k], gr.at[q, k, 3])
         weights, transposed = (wo, False) if q == 0 else (wi, True)
         product(sp.at[q, k], ag.at[q, k], weights, transposed)
@@ -231,8 +246,8 @@
     load_t.start()
 
     steps = {
-        "gm": gather_col_mid, "gc": gather_col_core, "rs": row_start, "rC": row_after_z, "rB": row_after_y,
-        "rE": row_end_z, "rF": row_end_y, "aA": gather_row_z, "aD": gather_row_y,
+        "gm": gather_col_mid, "gc": gather_col_core, "rs": row_start, "rA": row_relay, "rB": row_after_y,
+        "rC": row_after_z, "rE": row_end_z, "rF": row_end_y, "aB": gather_row_relay, "aD": gather_row_y,
         "cs": col_start, "cm": col_mid, "cz": col_z, "ce": col_end,
     }
     first = {"rs": [load_wi], "cs": [load_wo, load_t]}
@@ -254,12 +269,13 @@
             await_bytes(sz.at[q, k], cs.at[q, k, 0])
             await_bytes(sx.at[q, k], cs.at[q, k, 1])
             await_bytes(sc.at[q, k], cs.at[q, k, 2])
-            await_bytes(hz.at[q, k], rs.at[q, k, 0])
+            await_bytes(hr.at[q, k], rs.at[q, k, 0])
             await_bytes(hy.at[q, k], rs.at[q, k, 1])
-            await_bytes(hy2.at[q, k], rs.at[q, k, 2])
-            await_bytes(hz2.at[q, k], rs.at[q, k, 3])
-            await_bytes(hz2.at[q, k], gs.at[q, k, 0])
-            await_bytes(hy.at[q, k], gs.at[q, k, 1])
+            await_bytes(hz2.at[q, k], rs.at[q, k, 2])
+            await_bytes(hz.at[q, k], rs.at[q, k, 3])
+            await_bytes(hy2.at[q, k], rs.at[q, k, 4])
+            await_bytes(hy.at[q, k], gs.at[q, k, 0])
+            await_bytes(hr.at[q, k], gs.at[q, k, 1])
             await_bytes(hy2.at[q, k], gs.at[q, k, 2])
             await_bytes(hz.at[q, k], gs.at[q, k, 3])
             await_bytes(sc.at[q, k], ss.at[q, k, 0])
@@ -282,12 +298,14 @@
         pltpu.VMEM((tokens, D), BF16),
         pltpu.VMEM((D, H), BF16),
         pltpu.VMEM((H, D), BF16),
-        pltpu.VMEM((K, 2, RB, H), F32),
+        pltpu.VMEM((K, 2, 2, RB, CZ), F32),
+        pltpu.VMEM((K, 2, RB, CY), F32),
         pltpu.VMEM((2, K, 2, 2, 4, RB, H), BF16),
-        pltpu.VMEM((2, K, 4, RB, H), BF16),
-        pltpu.VMEM((2, K, 3, 2, RB, H), BF16),
-        pltpu.VMEM((2, K, RB, H), BF16),
-        pltpu.VMEM((2, K, 3, RB, H), BF16),
+        pltpu.VMEM((2, K, 2, 4, RB, CY), BF16),
+        pltpu.VMEM((2, K, 2, 2, RB, CZ), BF16),
+        pltpu.VMEM((2, K, 2, 2, 2, RB, CZ), BF16),
+        pltpu.VMEM((2, K, 2, 2, RB, CZ), BF16),
+        pltpu.VMEM((2, K, 3, 2, RB, CY), BF16),
         pltpu.VMEM((2, K, 2, 2, 4, RB, H), BF16),
         pltpu.VMEM((2, K, 2, 2, 4, RB, D), BF16),
         pltpu.VMEM((2, K, 2, 2, 4, RB, D), BF16),
@@ -295,7 +313,7 @@
         pltpu.VMEM((2, K, 3, 2, RB, D), BF16),
         pltpu.VMEM((2, K, RB, D), BF16),
         dma(K + 3), dma(2 + K),
-        dma(2, K, 3), dma(2, K, 3), dma(2, K, 4), dma(2, K, 4),
+        dma(2, K, 3), dma(2, K, 3), dma(2, K, 5), dma(2, K, 5),
         dma(2, K, 4), dma(2, K, 4), dma(2, K, 3), dma(2, K, 3),
     ]
     anywhere = pl.BlockSpec(memory_space=pl.ANY)

time: 167 us -> 156 us (0.934)
  Pallas kernels: 159 us -> 149 us
    pallas_call x1, Pallas kernels: 159 us -> 149 us  [shards(): pl.pallas_call(kernel, out_shape=(jax.ShapeDtypeStruct((tokens, D), BF16)...]
where the time goes in v4:
time: 156 us
  Pallas kernels  149 us (96%)
  local copies, waits for them, and re-layouts  6.1 us (4%)
    pallas_call x1, Pallas kernels, shards(): pl.pallas_call(kernel, out_shape=(jax.ShapeDtypeStruct((tokens, D), BF16)...  149 us
    unnamed x5, local copies, waits for them, and re-layouts  6.1 us

profile of v4, /device:TPU:0, one launch (start us, length us, event | category | flops | bytes accessed | tf_op | source)
XLA Modules:
  0.0 155.9 jit_solution(12428795665895417444)
XLA Ops:
  0.6 149.2 %shard_map.67 = (bf16[96,896]{1,0:T(8,128)(2,1)}, bf16[896,1152]{1,0:T(8,128)(2,1)}, bf16[1152,896]{1,0:T(8,128)(2,1)}) custom-call(bf16[96,896]{1,0:T(8,128)(2,1)} %x_hbm.1, bf16[96,896]{1,0:T(8,128)(2,1)} %t_hbm.1, bf16[896,1152]{1,0:T(8,128)(2,1)} %wi_hbm.1, bf16[1152,896]{1,0:T(8,128)(2,1)} %wo_hbm.1), custom_call_target="tpu_custom_call" | custom-call | tf_op jit(solution)/shard_map/pallas_call | solution.py:320
  149.8 1.6 %copy.10 = bf16[96,896]{1,0:T(8,128)(2,1)} copy(bf16[96,896]{1,0:T(8,128)(2,1)} %get-tuple-element.6) | data formatting | bytes 344064
  151.4 0.0 copy-start
  151.5 3.2 %copy.11 = bf16[896,1152]{1,0:T(8,128)(2,1)} copy(bf16[896,1152]{1,0:T(8,128)(2,1)} %get-tuple-element.7) | data formatting | bytes 4128768
  154.6 0.0 copy-done
  154.6 1.3 copy.12
Async XLA Ops:
  151.4 3.2 %copy-start = (bf16[1152,896]{1,0:T(8,128)(2,1)S(1)}, bf16[1152,896]{1,0:T(8,128)(2,1)}, u32[]{:S(2)}) copy-start(bf16[1152,896]{1,0:T(8,128)(2,1)} %get-tuple-element.8) | copy-start | bytes 6193156

commit v5 on v4

--- a/solution.py
+++ b/solution.py
@@ -16,27 +16,28 @@
 D = 896
 H = 1152
 HALF = 8 * RB
-CZ = 640
+CZ = 768
 CY = H - CZ
 
 ORDER = (
-    "A0gm", "A0gc", "E0gm", "D0gm", "A0rs", "C0gm", "E0gc", "D0gc", "A0rA", "B0gm",
-    "C0gc", "E0rs", "A0rC", "A0rB", "C0rs", "D0rs", "A0rF", "E0rA", "E0rC", "F0gm",
-    "B0gc", "B0rs", "D0rA", "A0rE", "A0aD", "D0rC", "B0rA", "C0rA", "B0rC", "D0rB",
-    "A0aB", "D0rF", "F0gc", "B0rB", "D0rE", "F0rs", "B0rF", "E0rB", "B0rE", "A0cs",
-    "D0aD", "F0rA", "D0aB", "B0aD", "A0cm", "E0rF", "E0rE", "B0aB", "D0cs", "C0rB",
-    "C0rC", "A0cz", "E0aD", "D0cm", "F0rC", "B0cs", "F0rB", "E0aB", "A0ce", "C0rF",
-    "B0cm", "D0cz", "C0rE", "E0cs", "F0rF", "A1gm", "C0aD", "D0ce", "F0rE", "B0cz",
-    "E0cm", "A1gc", "F0aD", "C0aB", "D1gm", "B0ce", "F0aB", "E0cz", "C0cs", "A1rs",
-    "B1gm", "D1gc", "E0ce", "C0cm", "F0cs", "B1gc", "D1rs", "F0cm", "A1rA", "B1rs",
-    "C0cz", "E1gm", "D1rC", "A1rC", "B1rA", "F0cz", "E1gc", "A1rB", "C0ce", "B1rC",
-    "F0ce", "E1rs", "C1gm", "A1rE", "A1rF", "F1gm", "B1rB", "C1gc", "B1rF", "E1rA",
-    "F1gc", "C1rs", "F1rs", "B1rE", "E1rC", "D1rA", "E1rB", "G", "C1rA", "B1aD",
-    "C1rC", "D1rB", "E1rF", "A1aB", "C1rB", "D1rF", "A1aD", "F1rA", "E1rE", "D1rE",
-    "D1aD", "B1aB", "C1rF", "A1cs", "F1rB", "F1rC", "D1aB", "E1aD", "A1cm", "C1rE",
-    "E1aB", "B1cs", "C1aD", "F1rF", "D1cs", "F1rE", "B1cm", "A1cz", "E1cs", "D1cm",
-    "C1aB", "F1aD", "F1aB", "E1cm", "C1cs", "B1cz", "F1cs", "D1cz", "C1cm", "A1ce",
-    "E1cz", "B1ce", "F1cm", "W", "C1cz", "D1ce", "F1cz", "C1ce", "E1ce", "F1ce",
+    "A0gs", "E0gs", "A0gm", "B0gs", "B0gm", "A0gc", "E0gm", "B0gc", "C0gs", "A0rs",
+    "E0gc", "B0rs", "E0rs", "D0gs", "C0gm", "A0rC", "F0gs", "B0rA", "B0rC", "D0gm",
+    "E0rA", "C0gc", "A0rA", "B0rB", "E0rC", "D0gc", "C0rs", "D0rs", "B0rF", "F0gm",
+    "B0rE", "A0rB", "A0rF", "D0rA", "B0aD", "C0rA", "E0rB", "E0rF", "A0rE", "D0rB",
+    "B0aB", "A0aD", "C0rB", "F0gc", "D0rC", "E0rE", "A0aB", "B0cs", "D0rF", "F0rs",
+    "C0rC", "E0aD", "A0cs", "B0cm", "E0aB", "A0cm", "C0rE", "D0aD", "C0rF", "E0cs",
+    "F0rA", "A0cz", "C0aB", "B0cz", "D0rE", "E0cm", "C0aD", "A0ce", "B0ce", "F0rC",
+    "F0rB", "C0cs", "D0aB", "A1gm", "B1gm", "E0cz", "F0rF", "C0cm", "F0rE", "D0cs",
+    "B1gc", "E0ce", "F0aD", "D0cm", "C0cz", "A1gc", "F0aB", "B1rs", "E1gm", "C0ce",
+    "A1rs", "D0cz", "F0cs", "B1rA", "E1gc", "B1rC", "C1gm", "F0cm", "A1rA", "D0ce",
+    "E1rs", "C1gc", "B1rF", "A1rC", "D1gm", "C1rs", "E1rA", "D1gc", "F0cz", "A1rB",
+    "E1rC", "C1rC", "D1rs", "F0ce", "C1rA", "E1rF", "B1rB", "A1rE", "A1rF", "F1gm",
+    "C1rF", "C1rB", "D1rA", "B1rE", "E1rB", "F1gc", "D1rC", "C1rE", "B1aD", "F1rs",
+    "D1rF", "D1rB", "B1aB", "E1rE", "A1aD", "G", "F1rA", "C1aD", "F1rC", "E1aD",
+    "C1aB", "B1cs", "E1aB", "F1rB", "D1rE", "A1aB", "B1cm", "C1cs", "F1rF", "E1cs",
+    "F1rE", "C1cm", "A1cs", "D1aD", "E1cm", "F1aD", "D1aB", "A1cm", "F1aB", "D1cs",
+    "C1cz", "F1cs", "E1cz", "D1cm", "B1cz", "A1cz", "F1cm", "W", "D1cz", "F1cz",
+    "C1ce", "A1ce", "E1ce", "B1ce", "D1ce", "F1ce",
 )
 
 
@@ -238,14 +239,16 @@
 
         lax.fori_loop(0, out.shape[0] // tile, step, 0)
 
-    for k in range(K):
-        loads[k].wait()
-        gather_col_start(0, k)
     load_wi.start()
     load_wo.start()
     load_t.start()
 
+    def gather_inputs(q, k):
+        loads[k].wait()
+        gather_col_start(q, k)
+
     steps = {
+        "gs": gather_inputs,
         "gm": gather_col_mid, "gc": gather_col_core, "rs": row_start, "rA": row_relay, "rB": row_after_y,
         "rC": row_after_z, "rE": row_end_z, "rF": row_end_y, "aB": gather_row_relay, "aD": gather_row_y,
         "cs": col_start, "cm": col_mid, "cz": col_z, "ce": col_end,
@@ -286,6 +289,25 @@
     for k in range(K):
         rows = pl.ds(k * RB, RB)
         pltpu.make_async_copy(gi.at[rows], gi_hbm.at[rows], osem.at[2 + k]).wait()
+
+
+def finish(a_in, b_in, c_in, a_out, b_out, c_out, a, b, c, sem):
+    moves = []
+    for i, (src, mid, dst, pieces) in enumerate(((b_in, b, b_out, 4), (c_in, c, c_out, 4), (a_in, a, a_out, 1))):
+        rows = src.shape[0] // pieces
+        for j in range(pieces):
+            at = pl.ds(j * rows, rows)
+            moves.append((
+                pltpu.make_async_copy(src.at[at], mid.at[at], sem.at[0, i, j]),
+                pltpu.make_async_copy(mid.at[at], dst.at[at], sem.at[1, i, j]),
+            ))
+    for load, _ in moves:
+        load.start()
+    for load, store in moves:
+        load.wait()
+        store.start()
+    for _, store in moves:
+        store.wait()
 
 
 def shards(inputs, teacher, weight_in, weight_out):
@@ -317,13 +339,14 @@
         dma(2, K, 4), dma(2, K, 4), dma(2, K, 3), dma(2, K, 3),
     ]
     anywhere = pl.BlockSpec(memory_space=pl.ANY)
-    return pl.pallas_call(
+    shapes = (
+        jax.ShapeDtypeStruct((tokens, D), BF16),
+        jax.ShapeDtypeStruct((D, H), BF16),
+        jax.ShapeDtypeStruct((H, D), BF16),
+    )
+    grads = pl.pallas_call(
         kernel,
-        out_shape=(
-            jax.ShapeDtypeStruct((tokens, D), BF16),
-            jax.ShapeDtypeStruct((D, H), BF16),
-            jax.ShapeDtypeStruct((H, D), BF16),
-        ),
+        out_shape=shapes,
         in_specs=[anywhere] * 4,
         out_specs=(anywhere,) * 3,
         scratch_shapes=scratch,
@@ -331,6 +354,14 @@
             collective_id=0, has_side_effects=True, vmem_limit_bytes=58 * 1024 * 1024
         ),
     )(inputs, teacher, weight_in, weight_out)
+    return pl.pallas_call(
+        finish,
+        out_shape=shapes,
+        in_specs=[anywhere] * 3,
+        out_specs=(anywhere,) * 3,
+        scratch_shapes=[pltpu.VMEM(shape.shape, BF16) for shape in shapes] + [dma(2, 3, 4)],
+        compiler_params=pltpu.CompilerParams(vmem_limit_bytes=58 * 1024 * 1024),
+    )(*grads)
 
 
 def solution(mesh):

time: 156 us -> 151 us (0.968)
  local copies, waits for them, and re-layouts: 6.1 us -> 0 us
    unnamed x5 -> x0, local copies, waits for them, and re-layouts: 6.1 us -> none
    pallas_call x1 -> x2, Pallas kernels: 149 us -> 150 us  [the longest x1 147 us: shards(): pl.pallas_call(kernel, out_shape=shapes, in_specs=[anywhere] * 4, out_spe...]
where the time goes in v5:
time: 151 us
  Pallas kernels  150 us (99%)
    pallas_call x1, Pallas kernels, shards(): pl.pallas_call(kernel, out_shape=shapes, in_specs=[anywhere] * 4, out_spe...  147 us
    pallas_call x1, Pallas kernels, shards(): pl.pallas_call(finish, out_shape=shapes, in_specs=[anywhere] * 3, out_spe...  3.63 us

profile of v5, /device:TPU:0, one launch (start us, length us, event | category | flops | bytes accessed | tf_op | source)
XLA Modules:
  0.0 151.1 jit_solution(3026294903460495931)
XLA Ops:
  0.6 146.7 %shard_map.67 = (bf16[96,896]{1,0:T(8,128)(2,1)}, bf16[896,1152]{1,0:T(8,128)(2,1)}, bf16[1152,896]{1,0:T(8,128)(2,1)}) custom-call(bf16[96,896]{1,0:T(8,128)(2,1)} %x_hbm.1, bf16[96,896]{1,0:T(8,128)(2,1)} %t_hbm.1, bf16[896,1152]{1,0:T(8,128)(2,1)} %wi_hbm.1, bf16[1152,896]{1,0:T(8,128)(2,1)} %wo_hbm.1), custom_call_target="tpu_custom_call" | custom-call | tf_op jit(solution)/shard_map/pallas_call | solution.py:347
  147.3 3.6 %shard_map.68 = (bf16[96,896]{1,0:T(8,128)(2,1)}, bf16[896,1152]{1,0:T(8,128)(2,1)}, bf16[1152,896]{1,0:T(8,128)(2,1)}) custom-call(bf16[96,896]{1,0:T(8,128)(2,1)} %get-tuple-element.6.a_in, bf16[896,1152]{1,0:T(8,128)(2,1)} %get-tuple-element.7.b_in, bf16[1152,896]{1,0:T(8,128)(2,1)} %get-tuple-element.8.c_in), custom_call_target="tpu_custom_call" | custom-call | tf_op jit(solution)/shard_map/pallas_call | solution.py:357

commit v6 on v5

--- a/solution.py
+++ b/solution.py
@@ -20,24 +20,24 @@
 CY = H - CZ
 
 ORDER = (
-    "A0gs", "E0gs", "A0gm", "B0gs", "B0gm", "A0gc", "E0gm", "B0gc", "C0gs", "A0rs",
-    "E0gc", "B0rs", "E0rs", "D0gs", "C0gm", "A0rC", "F0gs", "B0rA", "B0rC", "D0gm",
-    "E0rA", "C0gc", "A0rA", "B0rB", "E0rC", "D0gc", "C0rs", "D0rs", "B0rF", "F0gm",
-    "B0rE", "A0rB", "A0rF", "D0rA", "B0aD", "C0rA", "E0rB", "E0rF", "A0rE", "D0rB",
-    "B0aB", "A0aD", "C0rB", "F0gc", "D0rC", "E0rE", "A0aB", "B0cs", "D0rF", "F0rs",
-    "C0rC", "E0aD", "A0cs", "B0cm", "E0aB", "A0cm", "C0rE", "D0aD", "C0rF", "E0cs",
-    "F0rA", "A0cz", "C0aB", "B0cz", "D0rE", "E0cm", "C0aD", "A0ce", "B0ce", "F0rC",
-    "F0rB", "C0cs", "D0aB", "A1gm", "B1gm", "E0cz", "F0rF", "C0cm", "F0rE", "D0cs",
-    "B1gc", "E0ce", "F0aD", "D0cm", "C0cz", "A1gc", "F0aB", "B1rs", "E1gm", "C0ce",
-    "A1rs", "D0cz", "F0cs", "B1rA", "E1gc", "B1rC", "C1gm", "F0cm", "A1rA", "D0ce",
-    "E1rs", "C1gc", "B1rF", "A1rC", "D1gm", "C1rs", "E1rA", "D1gc", "F0cz", "A1rB",
-    "E1rC", "C1rC", "D1rs", "F0ce", "C1rA", "E1rF", "B1rB", "A1rE", "A1rF", "F1gm",
-    "C1rF", "C1rB", "D1rA", "B1rE", "E1rB", "F1gc", "D1rC", "C1rE", "B1aD", "F1rs",
-    "D1rF", "D1rB", "B1aB", "E1rE", "A1aD", "G", "F1rA", "C1aD", "F1rC", "E1aD",
-    "C1aB", "B1cs", "E1aB", "F1rB", "D1rE", "A1aB", "B1cm", "C1cs", "F1rF", "E1cs",
-    "F1rE", "C1cm", "A1cs", "D1aD", "E1cm", "F1aD", "D1aB", "A1cm", "F1aB", "D1cs",
-    "C1cz", "F1cs", "E1cz", "D1cm", "B1cz", "A1cz", "F1cm", "W", "D1cz", "F1cz",
-    "C1ce", "A1ce", "E1ce", "B1ce", "D1ce", "F1ce",
+    "A0gs", "E0gs", "A0gm", "E0gm", "F0gs", "C0gs", "A0gc", "F0gm", "E0gc", "A0rs",
+    "E0rs", "F0gc", "A0rA", "F0rs", "E0rA", "A0rB", "E0rC", "A0rC", "F0rA", "B0gs",
+    "E0rB", "F0rC", "C0gm", "E0rF", "A0rE", "B0gm", "C0gc", "D0gs", "E0rE", "E0aD",
+    "A0rF", "D0gm", "C0rs", "E0aB", "A0aB", "F0rB", "D0gc", "A0aD", "C0rA", "F0rF",
+    "D0rs", "B0gc", "E0cs", "F0rE", "E0cm", "B0rs", "A0cs", "C0rB", "C0rC", "A0cm",
+    "E0cz", "D0rA", "F0aD", "F0aB", "B0rA", "E0ce", "C0rF", "D0rC", "C0rE", "A0cz",
+    "D0rB", "F0cs", "B0rB", "B0rC", "E1gm", "F0cm", "C0aD", "A0ce", "D0rF", "C0aB",
+    "E1gc", "D0rE", "B0rE", "F0cz", "B0rF", "D0aD", "C0cs", "A1gm", "D0aB", "F0ce",
+    "E1rs", "C0cm", "B0aD", "A1gc", "B0aB", "F1gm", "D0cs", "E1rC", "E1rA", "C0cz",
+    "A1rs", "F1gc", "D0cm", "B0cs", "C0ce", "E1rF", "E1rB", "F1rs", "C1gm", "D0cz",
+    "B0cm", "A1rA", "A1rC", "E1rE", "C1gc", "F1rA", "A1rB", "D0ce", "F1rC", "A1rF",
+    "B0cz", "C1rs", "D1gm", "A1rE", "B0ce", "F1rF", "F1rB", "E1aB", "C1rA", "E1aD",
+    "C1rC", "D1gc", "B1gm", "D1rs", "F1rE", "B1gc", "A1aD", "A1aB", "E1cs", "D1rA",
+    "B1rs", "D1rC", "G1", "F1aD", "A1cs", "D1rB", "F1aB", "B1rA", "B1rC", "G2",
+    "C1rF", "C1rB", "D1rF", "F1cs", "B1rB", "E1cm", "D1rE", "A1cm", "F1cm", "C1rE",
+    "C1aD", "B1rF", "D1aD", "D1aB", "B1rE", "G0", "C1aB", "B1aD", "A1cz", "D1cs",
+    "B1aB", "C1cs", "D1cm", "A1ce", "E1cz", "B1cs", "C1cm", "B1cm", "D1cz", "W0",
+    "F1cz", "D1ce", "C1cz", "W2", "E1ce", "B1cz", "F1ce", "C1ce", "W1", "B1ce",
 )
 
 
@@ -226,7 +226,7 @@
             gi[rows, :] = total.astype(BF16)
             pltpu.make_async_copy(gi.at[rows], gi_hbm.at[rows], osem.at[2 + k]).start()
 
-    def weight_grad(out, left, right, tile):
+    def weight_grad(out, hbm, sem, left, right, tile, first, last):
         b = right.reshape(K * 2 * HALF, right.shape[-1])
         a = left.reshape(K * 2 * HALF, left.shape[-1])
 
@@ -237,7 +237,9 @@
             ).astype(BF16)
             return carry
 
-        lax.fori_loop(0, out.shape[0] // tile, step, 0)
+        lax.fori_loop(first, last, step, 0)
+        rows = pl.ds(first * tile, (last - first) * tile)
+        pltpu.make_async_copy(out.at[rows], hbm.at[rows], sem).start()
 
     load_wi.start()
     load_wo.start()
@@ -255,12 +257,12 @@
     }
     first = {"rs": [load_wi], "cs": [load_wo, load_t]}
     for event in ORDER:
-        if event == "G":
-            weight_grad(gwo, ag.at[0], xg.at[1], 384)
-            pltpu.make_async_copy(gwo, gwo_hbm, osem.at[1]).start()
-        elif event == "W":
-            weight_grad(gwi, xg.at[0], ag.at[1], 128)
-            pltpu.make_async_copy(gwi, gwi_hbm, osem.at[0]).start()
+        if event[0] == "G":
+            i = int(event[1])
+            weight_grad(gwo, gwo_hbm, osem.at[1], ag.at[0], xg.at[1], 384, i, i + 1)
+        elif event[0] == "W":
+            i = int(event[1])
+            weight_grad(gwi, gwi_hbm, osem.at[0], xg.at[0], ag.at[1], 128, (0, 3, 5)[i], (3, 5, 7)[i])
         else:
             k, q, step = ord(event[0]) - ord("A"), int(event[1]), event[2:]
             for load in first.pop(step, []):

time: 151 us -> 145 us (0.960)
  Pallas kernels: 150 us -> 144 us
    pallas_call x1, Pallas kernels: 147 us -> 141 us  [shards(): pl.pallas_call(kernel, out_shape=shapes, in_specs=[anywhere] * 4, out_spe...]
where the time goes in v6:
time: 145 us
  Pallas kernels  144 us (99%)
    pallas_call x1, Pallas kernels, shards(): pl.pallas_call(kernel, out_shape=shapes, in_specs=[anywhere] * 4, out_spe...  141 us
    pallas_call x1, Pallas kernels, shards(): pl.pallas_call(finish, out_shape=shapes, in_specs=[anywhere] * 3, out_spe...  3.63 us

profile of v6, /device:TPU:0, one launch (start us, length us, event | category | flops | bytes accessed | tf_op | source)
XLA Modules:
  0.0 145.0 jit_solution(17835050558022681115)
XLA Ops:
  0.6 140.6 %shard_map.67 = (bf16[96,896]{1,0:T(8,128)(2,1)}, bf16[896,1152]{1,0:T(8,128)(2,1)}, bf16[1152,896]{1,0:T(8,128)(2,1)}) custom-call(bf16[96,896]{1,0:T(8,128)(2,1)} %x_hbm.1, bf16[96,896]{1,0:T(8,128)(2,1)} %t_hbm.1, bf16[896,1152]{1,0:T(8,128)(2,1)} %wi_hbm.1, bf16[1152,896]{1,0:T(8,128)(2,1)} %wo_hbm.1), custom_call_target="tpu_custom_call" | custom-call | tf_op jit(solution)/shard_map/pallas_call | solution.py:349
  141.2 3.6 %shard_map.68 = (bf16[96,896]{1,0:T(8,128)(2,1)}, bf16[896,1152]{1,0:T(8,128)(2,1)}, bf16[1152,896]{1,0:T(8,128)(2,1)}) custom-call(bf16[96,896]{1,0:T(8,128)(2,1)} %get-tuple-element.6.a_in, bf16[896,1152]{1,0:T(8,128)(2,1)} %get-tuple-element.7.b_in, bf16[1152,896]{1,0:T(8,128)(2,1)} %get-tuple-element.8.c_in), custom_call_target="tpu_custom_call" | custom-call | tf_op jit(solution)/shard_map/pallas_call | solution.py:359

commit v7 on v6

--- a/solution.py
+++ b/solution.py
@@ -16,28 +16,28 @@
 D = 896
 H = 1152
 HALF = 8 * RB
-CZ = 768
+CZ = 640
 CY = H - CZ
 
 ORDER = (
-    "A0gs", "E0gs", "A0gm", "E0gm", "F0gs", "C0gs", "A0gc", "F0gm", "E0gc", "A0rs",
-    "E0rs", "F0gc", "A0rA", "F0rs", "E0rA", "A0rB", "E0rC", "A0rC", "F0rA", "B0gs",
-    "E0rB", "F0rC", "C0gm", "E0rF", "A0rE", "B0gm", "C0gc", "D0gs", "E0rE", "E0aD",
-    "A0rF", "D0gm", "C0rs", "E0aB", "A0aB", "F0rB", "D0gc", "A0aD", "C0rA", "F0rF",
-    "D0rs", "B0gc", "E0cs", "F0rE", "E0cm", "B0rs", "A0cs", "C0rB", "C0rC", "A0cm",
-    "E0cz", "D0rA", "F0aD", "F0aB", "B0rA", "E0ce", "C0rF", "D0rC", "C0rE", "A0cz",
-    "D0rB", "F0cs", "B0rB", "B0rC", "E1gm", "F0cm", "C0aD", "A0ce", "D0rF", "C0aB",
-    "E1gc", "D0rE", "B0rE", "F0cz", "B0rF", "D0aD", "C0cs", "A1gm", "D0aB", "F0ce",
-    "E1rs", "C0cm", "B0aD", "A1gc", "B0aB", "F1gm", "D0cs", "E1rC", "E1rA", "C0cz",
-    "A1rs", "F1gc", "D0cm", "B0cs", "C0ce", "E1rF", "E1rB", "F1rs", "C1gm", "D0cz",
-    "B0cm", "A1rA", "A1rC", "E1rE", "C1gc", "F1rA", "A1rB", "D0ce", "F1rC", "A1rF",
-    "B0cz", "C1rs", "D1gm", "A1rE", "B0ce", "F1rF", "F1rB", "E1aB", "C1rA", "E1aD",
-    "C1rC", "D1gc", "B1gm", "D1rs", "F1rE", "B1gc", "A1aD", "A1aB", "E1cs", "D1rA",
-    "B1rs", "D1rC", "G1", "F1aD", "A1cs", "D1rB", "F1aB", "B1rA", "B1rC", "G2",
-    "C1rF", "C1rB", "D1rF", "F1cs", "B1rB", "E1cm", "D1rE", "A1cm", "F1cm", "C1rE",
-    "C1aD", "B1rF", "D1aD", "D1aB", "B1rE", "G0", "C1aB", "B1aD", "A1cz", "D1cs",
-    "B1aB", "C1cs", "D1cm", "A1ce", "E1cz", "B1cs", "C1cm", "B1cm", "D1cz", "W0",
-    "F1cz", "D1ce", "C1cz", "W2", "E1ce", "B1cz", "F1ce", "C1ce", "W1", "B1ce",
+    "E0gs", "C0gs", "E0gm", "C0gm", "B0gs", "E0gc", "B0gm", "C0gc", "A0gs", "F0gs",
+    "D0gs", "E0rs", "B0gc", "C0rs", "E0rA", "B0rs", "D0gm", "E0rC", "C0rA", "A0gm",
+    "B0rA", "F0gm", "C0rC", "E0rB", "E0rF", "D0gc", "B0rB", "B0rC", "A0gc", "C0rB",
+    "E0rE", "C0rF", "E0aD", "B0rF", "E0aB", "B0rE", "A0rs", "B0aD", "C0rE", "E0cs",
+    "B0aB", "C0aD", "D0rs", "A0rA", "F0gc", "E0cm", "C0aB", "A0rC", "F0rs", "B0cs",
+    "E0cz", "D0rA", "C0cs", "A0rB", "B0cm", "A0rF", "F0rA", "D0rC", "F0rC", "E0ce",
+    "C0cm", "D0rB", "A0rE", "B0cz", "A0aD", "D0rF", "E1gm", "B0ce", "D0rE", "C0cz",
+    "F0rB", "A0aB", "F0rF", "E1gc", "B1gm", "C0ce", "D0aD", "D0aB", "E1rs", "A0cs",
+    "B1gc", "C1gm", "F0aD", "F0rE", "D0cs", "E1rA", "A0cm", "B1rs", "C1gc", "F0aB",
+    "E1rC", "D0cm", "C1rs", "A0cz", "F0cs", "B1rA", "B1rC", "D0cz", "E1rF", "E1rB",
+    "C1rA", "F0cm", "C1rC", "A0ce", "D0ce", "B1rB", "B1rF", "E1rE", "A1gm", "F0cz",
+    "D1gm", "C1rB", "C1rF", "B1rE", "A1gc", "F0ce", "E1aB", "E1aD", "C1rE", "D1gc",
+    "A1rs", "F1gm", "D1rs", "C1aD", "E1cs", "F1gc", "A1rA", "C1aB", "B1aB", "A1rC",
+    "A1rB", "E1cm", "D1rA", "F1rs", "D1rC", "A1rF", "G1", "D1rB", "F1rA", "C1cs",
+    "A1rE", "B1aD", "F1rC", "F1rB", "A1aD", "D1rE", "D1rF", "G0", "A1aB", "B1cs",
+    "F1rF", "C1cm", "F1rE", "D1aB", "E1cz", "D1aD", "B1cm", "A1cs", "F1aD", "F1aB",
+    "A1cm", "D1cs", "G2", "F1cs", "D1cm", "W1", "F1cm", "A1cz", "W2", "C1cz",
+    "D1cz", "B1cz", "W0", "F1cz", "A1ce", "B1ce", "C1ce", "E1ce", "D1ce", "F1ce",
 )
 
 

time: 145 us -> 142 us (0.979)
  Pallas kernels: 144 us -> 141 us
    pallas_call x1, Pallas kernels: 141 us -> 137 us  [shards(): pl.pallas_call(kernel, out_shape=shapes, in_specs=[anywhere] * 4, out_spe...]
where the time goes in v7:
time: 142 us
  Pallas kernels  141 us (99%)
    pallas_call x1, Pallas kernels, shards(): pl.pallas_call(kernel, out_shape=shapes, in_specs=[anywhere] * 4, out_spe...  137 us
    pallas_call x1, Pallas kernels, shards(): pl.pallas_call(finish, out_shape=shapes, in_specs=[anywhere] * 3, out_spe...  3.63 us

profile of v7, /device:TPU:0, one launch (start us, length us, event | category | flops | bytes accessed | tf_op | source)
XLA Modules:
  0.0 141.6 jit_solution(12173213235447173878)
XLA Ops:
  0.6 137.2 %shard_map.67 = (bf16[96,896]{1,0:T(8,128)(2,1)}, bf16[896,1152]{1,0:T(8,128)(2,1)}, bf16[1152,896]{1,0:T(8,128)(2,1)}) custom-call(bf16[96,896]{1,0:T(8,128)(2,1)} %x_hbm.1, bf16[96,896]{1,0:T(8,128)(2,1)} %t_hbm.1, bf16[896,1152]{1,0:T(8,128)(2,1)} %wi_hbm.1, bf16[1152,896]{1,0:T(8,128)(2,1)} %wo_hbm.1), custom_call_target="tpu_custom_call" | custom-call | tf_op jit(solution)/shard_map/pallas_call | solution.py:349
  137.8 3.6 %shard_map.68 = (bf16[96,896]{1,0:T(8,128)(2,1)}, bf16[896,1152]{1,0:T(8,128)(2,1)}, bf16[1152,896]{1,0:T(8,128)(2,1)}) custom-call(bf16[96,896]{1,0:T(8,128)(2,1)} %get-tuple-element.6.a_in, bf16[896,1152]{1,0:T(8,128)(2,1)} %get-tuple-element.7.b_in, bf16[1152,896]{1,0:T(8,128)(2,1)} %get-tuple-element.8.c_in), custom_call_target="tpu_custom_call" | custom-call | tf_op jit(solution)/shard_map/pallas_call | solution.py:359
